TPU v7x, 128 devices: a whole 4x4x4 slice. The times are simulated.
128 devices in a mesh: dp: 16 (over y, z), ctx: 8 (over x, core).
Axes of the slice: x: 4, y: 4, z: 4, core: 2. Of those that a mesh axis runs over, the one named last changes fastest.
Arguments:
- queries: bfloat16 [64, 8, 128, 4096], P('dp', 'ctx'), may hold values from -6 to 6
- key_rows: bfloat16 [64, 8, 128, 512], P('dp', 'ctx'), may hold values from -6 to 6
- bin_value_rows: bfloat16 [64, 8, 128, 512], P('dp', 'ctx'), may hold values from -6 to 6
- lengths: int32 [64, 3], P('dp'), may hold values from 1 to 1021, as said below
- routes: int32 [64, 1], replicated, may hold values from 0 to 15, as said below
Outputs:
- attended: bfloat16 [64, 8, 128, 4096], P('dp', 'ctx')
Inputs may be any that keep to these rules, and one draw needn't show every extreme that they name: `lengths`: every bin has a prompt of 2 or more positions and chosen and rejected responses of 1 or more; the three sum to at most 1024, with equality in some bin of every row. `routes`: rows are the aligned blocks of 4 bins. Each row sends its 4 bins to 4 different destination rows, and every destination row receives exactly 4 bins.
All inputs are finite; a program needn't handle non-finite values.
Results may differ from a plain program's by a relative error of at most 0.0039.
Values may be sent and summed in bfloat16 or wider, within the bound.
No kernel may reach another device: no remote copies, remote signals or barrier semaphores. Data moves between devices by JAX's collectives and lax.ppermute only.
A program may use at most 128 MiB of HBM per device.

v0:
```python
import math

import jax
import jax.numpy as jnp
from jax import lax
from jax.sharding import PartitionSpec as P

QUERY_HEADS = 32
KEY_VALUE_HEADS = 4
HEAD_SIZE = 128


def token_roles(lengths, positions):
    prompt = lengths[:, 0:1]
    chosen_len = lengths[:, 1:2]
    rejected_len = lengths[:, 2:3]
    places = positions[None, :]
    live = places < prompt + chosen_len + rejected_len
    chosen = (places >= prompt) & (places < prompt + chosen_len)
    rejected = (places >= prompt + chosen_len) & live
    return (live, chosen, rejected)


def visibility(lengths, query_pos, key_pos):
    live_q, chosen_q, reject_q = token_roles(lengths, query_pos)
    live_k, chosen_k, reject_k = token_roles(lengths, key_pos)
    causal = key_pos[None, None, :] <= query_pos[None, :, None]
    cross = (
        chosen_q[:, :, None] & reject_k[:, None, :] | reject_q[:, :, None] & chosen_k[:, None, :]
    )
    seen = causal & live_q[:, :, None] & live_k[:, None, :] & jnp.logical_not(cross)
    itself = jnp.logical_not(live_q)[:, :, None] & (
        key_pos[None, None, :] == query_pos[None, :, None]
    )
    return (seen | itself, live_q)


def attend(queries, key_all, value_all, lengths, ctx_index):
    item_count, _, block_width, features = queries.shape
    position_span = key_all.shape[1] * block_width
    head_groups = QUERY_HEADS // KEY_VALUE_HEADS
    loop_step = math.gcd(item_count, max(1, 256 // block_width))
    query_pos = ctx_index * block_width + jnp.arange(block_width, dtype=jnp.int32)
    key_pos = jnp.arange(position_span, dtype=jnp.int32)
    scale_factor = 1.0 / math.sqrt(HEAD_SIZE)

    def one_block(block):
        query_block, key_block, value_block, len_blk = block
        query_heads = query_block.reshape(
            loop_step, block_width, KEY_VALUE_HEADS, head_groups, HEAD_SIZE
        )
        key_heads = key_block.reshape(loop_step, position_span, KEY_VALUE_HEADS, HEAD_SIZE)
        value_heads = value_block.reshape(loop_step, position_span, KEY_VALUE_HEADS, HEAD_SIZE)
        scores = (
            jnp.einsum(
                "bqhgd,bkhd->bhgqk", query_heads, key_heads, preferred_element_type=jnp.float32
            )
            * scale_factor
        )
        seen, live_q = visibility(len_blk, query_pos, key_pos)
        seen_b = seen[:, None, None]
        top = jnp.max(jnp.where(seen_b, scores, -1e30), axis=-1, keepdims=True)
        weights = jnp.where(seen_b, jnp.exp(scores - top), 0.0)
        total = jnp.sum(weights, axis=-1)
        rounded = weights.astype(jnp.bfloat16)
        mixed = jnp.einsum(
            "bhgqk,bkhd->bqhgd", rounded, value_heads, preferred_element_type=jnp.float32
        )
        mixed = mixed / jnp.transpose(total, (0, 3, 1, 2))[..., None]
        mixed = jnp.where(live_q[:, :, None, None, None], mixed, 0.0)
        return mixed.astype(jnp.bfloat16).reshape(loop_step, 1, block_width, features)

    blocks = (
        queries.reshape(item_count // loop_step, loop_step, 1, block_width, features),
        key_all.reshape(
            item_count // loop_step, loop_step, key_all.shape[1], block_width, key_all.shape[3]
        ),
        value_all.reshape(
            item_count // loop_step, loop_step, value_all.shape[1], block_width, value_all.shape[3]
        ),
        lengths.reshape(item_count // loop_step, loop_step, 3),
    )
    return lax.map(one_block, blocks).reshape(item_count, 1, block_width, features)


def arrange(table, arrays):
    return jnp.einsum(
        "sb,bcwf->scwf", table.astype(jnp.bfloat16), arrays, preferred_element_type=jnp.float32
    ).astype(jnp.bfloat16)


def arrange_ints(table, lengths):
    return jnp.sum(jnp.where(table[:, :, None], lengths[None, :, :], 0), axis=1).astype(jnp.int32)


def shards(queries, key_rows, bin_value_rows, lengths, routes):
    bins = queries.shape[0]
    rows = lax.axis_size("dp")
    my_row = lax.axis_index("dp")
    all_routes = routes[:, 0]
    own_routes = lax.dynamic_slice_in_dim(all_routes, my_row * bins, bins)
    send_table = jnp.arange(rows, dtype=jnp.int32)[:, None] == own_routes[None, :]
    grid = all_routes.reshape(rows, bins)
    sends_here = jnp.sum((grid == my_row).astype(jnp.int32), axis=1)
    arrival = jnp.cumsum(sends_here) - sends_here
    place_table = (jnp.arange(bins, dtype=jnp.int32)[:, None] == arrival[None, :]) & (
        sends_here[None, :] > 0
    )
    ctx_index = lax.axis_index("ctx")
    moved_q, moved_k, moved_v, moved_len = (
        lax.all_to_all(arrange(send_table, queries), "dp", split_axis=0, concat_axis=0, tiled=True),
        lax.all_to_all(
            arrange(send_table, key_rows), "dp", split_axis=0, concat_axis=0, tiled=True
        ),
        lax.all_to_all(
            arrange(send_table, bin_value_rows), "dp", split_axis=0, concat_axis=0, tiled=True
        ),
        lax.all_to_all(
            arrange_ints(send_table, lengths), "dp", split_axis=0, concat_axis=0, tiled=True
        ),
    )
    slot_q = arrange(place_table, moved_q)
    slot_k = arrange(place_table, moved_k)
    slot_v = arrange(place_table, moved_v)
    slot_len = arrange_ints(place_table, moved_len)
    key_all, value_all = (
        lax.all_gather(slot_k, "ctx", axis=1, tiled=True),
        lax.all_gather(slot_v, "ctx", axis=1, tiled=True),
    )
    attended = attend(slot_q, key_all, value_all, slot_len, ctx_index)
    return attended


def solution(mesh):
    in_specs = (
        P("dp", "ctx", None, None),
        P("dp", "ctx", None, None),
        P("dp", "ctx", None, None),
        P("dp", None),
        P(),
    )
    out_specs = P("dp", "ctx", None, None)
    return jax.shard_map(shards, mesh=mesh, in_specs=in_specs, out_specs=out_specs, check_vma=False)
```

profile of v0, /device:TPU:4, one launch (start us, length us, event | category | flops | bytes accessed | tf_op | source)
XLA Modules:
  0.0 539.0 jit_solution(4319648979331545438)
XLA Ops:
  8.9 8.0 %all-to-all-start = ((s32[16,1,3]{2,1,0:T(1,128)}), s32[16,1,3]{2,1,0:T(1,128)S(1)}, u32[]{:S(2)}, u32[]{:S(2)}) async-start(s32[16,1,3]{2,1,0:T(1,128)} %copy.56), calls=%async_computation | async-start | bytes 16384 | tf_op jit(solution)/shard_map/all_to_all | solution.py:118
  20.4 4.2 all-to-all-done
  24.6 3.7 all-to-all-start.1
  31.7 25.1 %all-to-all-done.1 = bf16[16,1,128,512]{3,2,1,0:T(8,128)(2,1)S(1)} async-done(((bf16[16,1,128,512]{3,2,1,0:T(8,128)(2,1)}), bf16[16,1,128,512]{3,2,1,0:T(8,128)(2,1)S(1)}, u32[]{:S(2)}, u32[]{:S(2)}) %all-to-all-start.1) | async-done | bytes 2097184 | tf_op jit(solution)/shard_map/all_to_all | solution.py:115
  56.8 4.4 all-to-all-start.2
  61.3 11.1 %convert_bitcast_fusion = bf16[16,1,128,4096]{3,0,2,1:T(8,128)(2,1)} fusion(bf16[4,128,4096]{2,1,0:T(8,128)(2,1)} %bitcast.153, s32[4]{0:T(128)S(1)} %dynamic-slice_bitcast_fusion), kind=kOutput, calls=%fused_computation.55 | convolution fusion | flops 75497536 | bytes 20971536 | tf_op jit(solution)/shard_map/sb,bcwf->scwf/dot_general | solution.py:87
  72.3 18.5 %copy.66 = bf16[16,1,128,4096]{3,2,1,0:T(8,128)(2,1)} copy(bf16[16,1,128,4096]{3,0,2,1:T(8,128)(2,1)} %convert_bitcast_fusion) | data formatting | bytes 33554432 | tf_op jit(solution)/shard_map/convert_element_type | solution.py:89
  90.8 7.3 %all-to-all-start.3 = ((bf16[16,1,128,4096]{3,2,1,0:T(8,128)(2,1)}), bf16[16,1,128,4096]{3,2,1,0:T(8,128)(2,1)}, u32[]{:S(2)}, u32[]{:S(2)}) async-start(bf16[16,1,128,4096]{3,2,1,0:T(8,128)(2,1)} %copy.66), calls=%async_computation.3 | async-start | bytes 33554432 | tf_op jit(solution)/shard_map/all_to_all | solution.py:111
  100.8 10.8 %all-gather.7.cloned.1.call-start = ((), (), s32[]{:S(2)}) async-start(), calls=%async_computation.5 | async-start | bytes 4718592 | tf_op jit(solution)/shard_map/all_gather | solution.py:127
  111.6 3.8 fusion.64
  115.8 17.4 %all-gather.5.cloned.1.call-done = bf16[4,1024,512]{2,0,1:T(4,128)(2,1)} async-done(((bf16[4,128,512]{2,0,1:T(4,128)(2,1)}), bf16[4,1024,512]{2,0,1:T(4,128)(2,1)}) %all-gather.5.cloned.1.call-update) | async-done | bytes 4194320 | tf_op jit(solution)/shard_map/all_gather | solution.py:128
  133.2 9.3 %reshape.526 = bf16[2,2,8,128,512]{4,1,0,3,2:T(2,128)(2,1)} reshape(bf16[4,1024,512]{2,0,1:T(4,128)(2,1)} %all-gather.5.cloned.1.call-done) | data formatting | bytes 8388608 | tf_op jit(solution)/shard_map/reshape | solution.py:78
  142.5 24.5 %all-gather.7.cloned.1.call-done = bf16[4,1024,512]{2,0,1:T(4,128)(2,1)} async-done(((bf16[4,128,512]{2,0,1:T(4,128)(2,1)}), bf16[4,1024,512]{2,0,1:T(4,128)(2,1)}) %all-gather.7.cloned.1.call-update) | async-done | bytes 4194320 | tf_op jit(solution)/shard_map/all_gather | solution.py:127
  167.0 9.3 %reshape.529 = bf16[2,2,8,128,512]{4,1,0,3,2:T(2,128)(2,1)} reshape(bf16[4,1024,512]{2,0,1:T(4,128)(2,1)} %all-gather.7.cloned.1.call-done) | data formatting | bytes 8388608 | tf_op jit(solution)/shard_map/reshape | solution.py:75
  176.3 197.4 %all-to-all-done.3 = bf16[16,1,128,4096]{3,2,1,0:T(8,128)(2,1)} async-done(((bf16[16,1,128,4096]{3,2,1,0:T(8,128)(2,1)}), bf16[16,1,128,4096]{3,2,1,0:T(8,128)(2,1)}, u32[]{:S(2)}, u32[]{:S(2)}) %all-to-all-start.3) | async-done | bytes 16777248 | tf_op jit(solution)/shard_map/all_to_all | solution.py:111
  373.7 26.8 %fusion.51 = bf16[4,128,4096]{2,0,1:T(4,128)(2,1)} fusion(bf16[16,1,128,4096]{3,2,1,0:T(8,128)(2,1)} %all-to-all-done.3, pred[4,16]{1,0:T(4,128)(4,1)S(1)} %fusion.69), kind=kOutput, calls=%fused_computation.56 | convolution fusion | flops 69206016 | bytes 20971584 | tf_op jit(solution)/shard_map/sb,bcwf->scwf/dot_general | solution.py:87
  400.5 7.9 %copy.76 = bf16[4,128,4096]{1,2,0:T(8,128)(2,1)} copy(bf16[4,128,4096]{2,0,1:T(4,128)(2,1)} %fusion.51) | data formatting | bytes 8388608
  408.4 122.5 %while.12 = (s32[]{:T(128)}, bf16[2,2,1,128,4096]{4,3,1,0,2:T(8,128)(2,1)}, s32[2,2,3]{2,1,0:T(2,128)S(1)}, bf16[2,2,8,128,512]{4,1,0,3,2:T(2,128)(2,1)}, bf16[2...) while((s32[]{:T(128)}, ...), condition=%wide.region_7.8_spmd.clone.clone, body=%wide.region_4.7_spmd.clone.clone.sunk | while | flops 10843873280 | bytes 60113680 | solution.py:83
  410.5 7.4 %constant_dynamic-slice_fusion.7 = (bf16[1,2,8,128,512]{4,1,0,3,2:T(2,128)(2,1)}, bf16[1,2,8,128,512]{4,1,0,3,2:T(2,128)(2,1)}) fusion(bf16[2,2,8,128,512]{4,1,0,3,2:T(2,128)(2,1)} %get-tuple-element.249, s32[]{:T(128)} %get-tuple-element.237, bf16[2,2,8,128,512]{4,1,0,3,2:T(2,128)(2,1)} %get-tuple-element.248), kind=kLoop, calls=%fused_computation.36.clone.1 | loop fusion | bytes 8388612 | tf_op jit(solution)/shard_map/while/body/jit(dynamic_index_in_dim)/dynamic_slice | solution.py:83
  427.5 14.7 %fusion.114 = f32[2,4,8,128]{3,2,1,0:T(8,128)S(1)} fusion(pred[2,128,1024]{1,2,0:T(8,128)(4,1)S(1)} %and_or_fusion.2, bf16[2,128,4,8,128]{1,4,3,2,0:T(8,128)(2,1)} %bitcast.149, bf16[2,1024,4,128]{1,3,2,0:T(8,128)(2,1)S(1)} %copy-done.2), kind=kOutput, calls=%fused_computation.85.clone.1 | convolution fusion | flops 4345299968 | bytes 4489216 | tf_op jit(solution)/shard_map/while/body/eval_jaxpr/sub | solution.py:63
  448.4 17.0 %fusion.115 = bf16[2,128,4,8,128]{1,4,3,2,0:T(8,128)(2,1)} fusion(pred[2,128,1024]{1,2,0:T(8,128)(4,1)S(1)} %and_or_fusion.2, bf16[2,128,4,8,128]{1,4,3,2,0:T(8,128)(2,1)} %bitcast.150, bf16[2,1024,4,128]{1,3,2,0:T(8,128)(2,1)} %copy.112, bf16[2,1024,4,128,1]{1,3,2,0,4:T(8,128)(2,1)} %copy.113, f32[2,128,4,8]{1,3,2,0:T(8,128)S(1)} %bitcast.159, ...), kind=kOutput, calls=%fused_computation.16.clone.1 | convolution fusion | flops 6495937536 | bytes 8683776 | tf_op jit(solution)/shard_map/while/body/eval_jaxpr/bhgqk,bkhd->bqhgd/dot_general | solution.py:66
  471.6 7.4 %constant_dynamic-slice_fusion.7 = (bf16[1,2,8,128,512]{4,1,0,3,2:T(2,128)(2,1)}, bf16[1,2,8,128,512]{4,1,0,3,2:T(2,128)(2,1)}) fusion(bf16[2,2,8,128,512]{4,1,0,3,2:T(2,128)(2,1)} %get-tuple-element.249, s32[]{:T(128)} %get-tuple-element.237, bf16[2,2,8,128,512]{4,1,0,3,2:T(2,128)(2,1)} %get-tuple-element.248), kind=kLoop, calls=%fused_computation.36.clone.1 | loop fusion | bytes 8388612 | tf_op jit(solution)/shard_map/while/body/jit(dynamic_index_in_dim)/dynamic_slice | solution.py:83
  488.5 14.8 %fusion.114 = f32[2,4,8,128]{3,2,1,0:T(8,128)S(1)} fusion(pred[2,128,1024]{1,2,0:T(8,128)(4,1)S(1)} %and_or_fusion.2, bf16[2,128,4,8,128]{1,4,3,2,0:T(8,128)(2,1)} %bitcast.149, bf16[2,1024,4,128]{1,3,2,0:T(8,128)(2,1)S(1)} %copy-done.2), kind=kOutput, calls=%fused_computation.85.clone.1 | convolution fusion | flops 4345299968 | bytes 4489216 | tf_op jit(solution)/shard_map/while/body/eval_jaxpr/sub | solution.py:63
  509.5 17.0 %fusion.115 = bf16[2,128,4,8,128]{1,4,3,2,0:T(8,128)(2,1)} fusion(pred[2,128,1024]{1,2,0:T(8,128)(4,1)S(1)} %and_or_fusion.2, bf16[2,128,4,8,128]{1,4,3,2,0:T(8,128)(2,1)} %bitcast.150, bf16[2,1024,4,128]{1,3,2,0:T(8,128)(2,1)} %copy.112, bf16[2,1024,4,128,1]{1,3,2,0,4:T(8,128)(2,1)} %copy.113, f32[2,128,4,8]{1,3,2,0:T(8,128)S(1)} %bitcast.159, ...), kind=kOutput, calls=%fused_computation.16.clone.1 | convolution fusion | flops 6495937536 | bytes 8683776 | tf_op jit(solution)/shard_map/while/body/eval_jaxpr/bhgqk,bkhd->bqhgd/dot_general | solution.py:66
  (69 shorter events, 56.7 us)
Async XLA Ops:
  6.5 10.5 %copy-start = (bf16[4,1,128,512]{3,2,1,0:T(8,128)(2,1)S(1)}, bf16[4,1,128,512]{3,2,1,0:T(8,128)(2,1)}, u32[]{:S(2)}) copy-start(bf16[4,1,128,512]{3,2,1,0:T(8,128)(2,1)} %param.9) | copy-start | bytes 1572868
  8.9 15.6 %all-to-all-start = ((s32[16,1,3]{2,1,0:T(1,128)}), s32[16,1,3]{2,1,0:T(1,128)S(1)}, u32[]{:S(2)}, u32[]{:S(2)}) async-start(s32[16,1,3]{2,1,0:T(1,128)} %copy.56), calls=%async_computation | async-start | bytes 16384 | tf_op jit(solution)/shard_map/all_to_all | solution.py:118
  17.9 10.4 %copy-start.3 = (bf16[4,1,128,512]{3,2,1,0:T(8,128)(2,1)S(1)}, bf16[4,1,128,512]{3,2,1,0:T(8,128)(2,1)}, u32[]{:S(2)}) copy-start(bf16[4,1,128,512]{3,2,1,0:T(8,128)(2,1)} %param.8) | copy-start | bytes 1572868
  24.6 32.3 %all-to-all-start.1 = ((bf16[16,1,128,512]{3,2,1,0:T(8,128)(2,1)}), bf16[16,1,128,512]{3,2,1,0:T(8,128)(2,1)S(1)}, u32[]{:S(2)}, u32[]{:S(2)}) async-start(bf16[16,1,128,512]{3,2,1,0:T(8,128)(2,1)} %copy.60), calls=%async_computation.1 | async-start | bytes 4194304 | tf_op jit(solution)/shard_map/all_to_all | solution.py:115
  56.8 34.0 %all-to-all-start.2 = ((bf16[16,1,128,512]{3,2,1,0:T(8,128)(2,1)}), bf16[16,1,128,512]{3,2,1,0:T(8,128)(2,1)}, u32[]{:S(2)}, u32[]{:S(2)}) async-start(bf16[16,1,128,512]{3,2,1,0:T(8,128)(2,1)} %copy.63), calls=%async_computation.2 | async-start | bytes 4194304 | tf_op jit(solution)/shard_map/all_to_all | solution.py:112
  90.8 7.3 %copy-start.4 = (s32[64,1]{0,1:T(1,128)S(1)}, s32[64,1]{0,1:T(1,128)}, u32[]{:S(2)}) copy-start(s32[64,1]{0,1:T(1,128)} %param.11) | copy-start | bytes 772
  90.8 282.9 %all-to-all-start.3 = ((bf16[16,1,128,4096]{3,2,1,0:T(8,128)(2,1)}), bf16[16,1,128,4096]{3,2,1,0:T(8,128)(2,1)}, u32[]{:S(2)}, u32[]{:S(2)}) async-start(bf16[16,1,128,4096]{3,2,1,0:T(8,128)(2,1)} %copy.66), calls=%async_computation.3 | async-start | bytes 33554432 | tf_op jit(solution)/shard_map/all_to_all | solution.py:111
  98.1 35.1 %all-gather.5.cloned.1.call-start = ((), (), s32[]{:S(2)}) async-start(), calls=%async_computation.4 | async-start | bytes 4718592 | tf_op jit(solution)/shard_map/all_gather | solution.py:128
  100.8 66.2 %all-gather.7.cloned.1.call-start = ((), (), s32[]{:S(2)}) async-start(), calls=%async_computation.5 | async-start | bytes 4718592 | tf_op jit(solution)/shard_map/all_gather | solution.py:127
  424.3 3.2 copy-start.2
  485.3 3.2 copy-start.2
  530.9 1.0 copy-start.1
Sparse Core Ops, SparseCore 0:
  100.9 32.2 all-gather.4
  134.9 32.0 all-gather.6
where the time goes:
time: 549 us; the launch traced here: 539 us
  waiting for transfers between devices  269 us (49%)
  local copies, waits for them, and re-layouts  109 us (20%)
  matrix products  109 us (20%)
  starting transfers between devices  34.3 us (6%)
  between operations  13.7 us (2%)
    all_to_all x1, waiting for transfers between devices, shards(): lax.all_to_all(arrange(send_table, queries), 'dp', split_axis=0, concat_a...  197 us
    dot_general x6, matrix products, arrange(): jnp.einsum('sb,bcwf->scwf', table.astype(jnp.bfloat16), arrays, preferred...  45.5 us
    dot_general x2, matrix products, one_block(): jnp.einsum('bhgqk,bkhd->bqhgd', rounded, value_heads, preferred_element_t...  34.1 us
    sub x2, matrix products, one_block(): weights = jnp.where(seen_b, jnp.exp(scores - top), 0.0)  29.5 us
    all_to_all x1, waiting for transfers between devices, shards(): lax.all_to_all(arrange(send_table, bin_value_rows), 'dp', split_axis=0, c...  25.1 us
    all_gather x1, waiting for transfers between devices, shards(): lax.all_gather(slot_k, 'ctx', axis=1, tiled=True)  24.5 us
    convert_element_type x3, local copies, waits for them, and re-layouts, arrange(): return jnp.einsum('sb,bcwf->scwf', table.astype(jnp.bfloat16), arrays, pr...  23.5 us
    dynamic_slice x4, local copies, waits for them, and re-layouts, attend(): lax.map(one_block, blocks).reshape(item_count, 1, block_width, features)  21.3 us
  transfers between devices with their start and end apart: 6, of which 5 were waited for; matrix products, arithmetic and copies ran while one was open for 11% of the time, Pallas kernels for 0%

commit v1 on v0

v1 whole, which is shorter than its diff:
```python
import functools
import math

import jax
import jax.numpy as jnp
from jax import lax
from jax.experimental import pallas as pl
from jax.experimental.pallas import tpu as pltpu
from jax.sharding import PartitionSpec as P

BINS = 4
ROWS = 16
CHIPS = 4
WIDTH = 128
HEAD = 128
GROUP = 8
PIECE = 16
PARTS = WIDTH // PIECE
HALF = GROUP // 2
NEG = -1e30
BF16 = jnp.bfloat16


def blocks(count):
    return jax.ShapeDtypeStruct((ROWS, count, PIECE, HEAD), BF16)


def pack_kernel(lengths, q_ref, k_ref, v_ref, u_ref, q_buf, k_buf, v_buf, u_buf, in_sems, out_sems):
    def arrive(b):
        wide, narrow = pl.ds(0, GROUP * HEAD), pl.ds(0, HEAD)
        return [
            pltpu.make_async_copy(q_ref.at[b, 0, :, wide], q_buf.at[b], in_sems.at[0, b]),
            pltpu.make_async_copy(k_ref.at[b, 0, :, narrow], k_buf.at[b], in_sems.at[1, b]),
            pltpu.make_async_copy(v_ref.at[b, 0, :, narrow], v_buf.at[b], in_sems.at[2, b]),
        ]

    def leave(i):
        part = pl.ds(i * HALF, HALF if i < BINS else BINS + 1)
        return pltpu.make_async_copy(u_buf.at[:, part], u_ref.at[:, part], out_sems.at[i])

    for b in range(BINS):
        for copy in arrive(b):
            copy.start()
    lane = lax.broadcasted_iota(jnp.int32, (PIECE, HEAD), 1)
    digits = jnp.zeros((PIECE, HEAD), jnp.int32)
    for i in range(3 * BINS):
        digits = jnp.where(lane == i, lengths[i] // 32, digits)
        digits = jnp.where(lane == 3 * BINS + i, lengths[i] % 32, digits)
    digits = digits.astype(jnp.float32).astype(BF16)
    for b in range(BINS):
        for copy in arrive(b):
            copy.wait()
        for j in range(ROWS):
            rows = pl.ds((j // 2) * PIECE, PIECE)
            for n in range(HALF):
                u_buf[j, b * HALF + n] = q_buf[b, rows, pl.ds(((j % 2) * HALF + n) * HEAD, HEAD)]
            u_buf[j, BINS * HALF + b] = (k_buf if j % 2 == 0 else v_buf)[b, rows]
            if b == 0:
                u_buf[j, BINS * HALF + BINS] = digits
        leave(b).start()
    leave(BINS).start()
    for i in range(BINS + 1):
        leave(i).wait()


def pack(lengths, queries, key_rows, value_rows):
    hbm = pl.BlockSpec(memory_space=pltpu.HBM)
    count = BINS * HALF + BINS + 1
    return pl.pallas_call(
        pack_kernel,
        grid_spec=pltpu.PrefetchScalarGridSpec(
            num_scalar_prefetch=1,
            grid=(),
            in_specs=[hbm] * 3,
            out_specs=hbm,
            scratch_shapes=[
                pltpu.VMEM((BINS, WIDTH, GROUP * HEAD), BF16),
                pltpu.VMEM((BINS, WIDTH, HEAD), BF16),
                pltpu.VMEM((BINS, WIDTH, HEAD), BF16),
                pltpu.VMEM((ROWS, count, PIECE, HEAD), BF16),
                pltpu.SemaphoreType.DMA((3, BINS)),
                pltpu.SemaphoreType.DMA((BINS + 1,)),
            ],
        ),
        out_shape=blocks(count),
        cost_estimate=pl.CostEstimate(flops=0, bytes_accessed=4 << 20, transcendentals=0),
        name="pack",
    )(lengths, queries, key_rows, value_rows)


def attend_kernel(from_pieces, to_pieces, scalars, q_ref, *refs):
    kv_refs, (out_ref, buffer, sems) = refs[: 2 * CHIPS], refs[2 * CHIPS :]
    item, head_at = pl.program_id(0), pl.program_id(1)
    ctx = scalars[3 * BINS]
    chip, core = ctx // 2, ctx % 2
    prompt = scalars[3 * item]
    split = prompt + scalars[3 * item + 1]
    end = split + scalars[3 * item + 2]
    start = ctx * WIDTH
    factor = math.log2(math.e) / math.sqrt(HEAD)

    def copy(i, b):
        return pltpu.make_async_copy(kv_refs[i].at[:, b], buffer.at[i, b], sems.at[i, b])

    @pl.when((item == 0) & (head_at == 0))
    def _():
        for b in range(BINS):
            for i in range(2 * CHIPS):

                @pl.when(i // 2 <= chip)
                def _(i=i, b=b):
                    copy(i, b).start()

    @pl.when(head_at == 0)
    def _():
        for i in range(2 * CHIPS):

            @pl.when(i // 2 <= chip)
            def _(i=i):
                copy(i, item).wait()

    def read_head(head):
        if not from_pieces:
            return q_ref[0, 0, :, pl.ds(head * HEAD, HEAD)]
        return jnp.concatenate([q_ref[2 * r + head // HALF, head % HALF] for r in range(PARTS)], axis=0)

    def write_head(head, rows):
        if to_pieces:
            for r in range(PARTS):
                out_ref[2 * r + head // HALF, head % HALF] = rows[r * PIECE : (r + 1) * PIECE]
        else:
            out_ref[0, 0, :, pl.ds(head * HEAD, HEAD)] = rows

    def attend(chips):
        keys = jnp.concatenate([buffer[i, item, 2 * head_at] for i in range(2 * chips)], axis=0)
        values = jnp.concatenate([buffer[i, item, 2 * head_at + 1] for i in range(2 * chips)], axis=0)
        t = start + lax.broadcasted_iota(jnp.int32, (WIDTH, WIDTH), 0)
        biases = []
        for i in range(2 * chips):
            origin = 2 * (chip - i // 2) + (core if i % 2 == 0 else 1 - core)
            u = origin * WIDTH + lax.broadcasted_iota(jnp.int32, (WIDTH, WIDTH), 1)
            hidden = (u > t) | ((t >= split) & (u >= prompt) & (u < split))
            biases.append(jnp.where(hidden, NEG, 0.0))
        bias = jnp.concatenate(biases, axis=1)
        live = (start + lax.broadcasted_iota(jnp.int32, (WIDTH, 1), 0)) < end
        bias = jnp.concatenate([bias, bias], axis=0)
        live = jnp.concatenate([live, live], axis=0)
        n = GROUP // 2
        qs = [jnp.concatenate([read_head(2 * i), read_head(2 * i + 1)], axis=0) for i in range(n)]
        scores = [lax.dot_general(q, keys, (((1,), (1,)), ((), ())), preferred_element_type=jnp.float32) + bias for q in qs]
        tops = [jnp.max(x, axis=1, keepdims=True) for x in scores]
        weights = [jnp.exp2((x - top) * factor) for x, top in zip(scores, tops)]
        wide = jnp.concatenate([values, jnp.ones_like(values)], axis=1)
        mixed = [jnp.dot(x.astype(BF16), wide, preferred_element_type=jnp.float32) for x in weights]
        for i in range(n):
            out = (mixed[i][:, :HEAD] * jnp.where(live, 1.0 / mixed[i][:, HEAD:], 0.0)).astype(BF16)
            write_head(2 * i, out[:WIDTH])
            write_head(2 * i + 1, out[WIDTH:])

    @pl.when(end <= start)
    def _():
        out_ref[...] = jnp.zeros_like(out_ref)

    for chips in range(1, CHIPS + 1):

        @pl.when((end > start) & (chip == chips - 1))
        def _(chips=chips):
            attend(chips)


def attend(scalars, q, kv, heads, q_spec, out_spec, out_shape, from_pieces, to_pieces, name):
    pairs = BINS * heads * GROUP * WIDTH * WIDTH * 2 * CHIPS
    return pl.pallas_call(
        functools.partial(attend_kernel, from_pieces, to_pieces),
        grid_spec=pltpu.PrefetchScalarGridSpec(
            num_scalar_prefetch=1,
            grid=(BINS, heads),
            in_specs=[q_spec] + [pl.BlockSpec(memory_space=pltpu.HBM)] * (2 * CHIPS),
            out_specs=out_spec,
            scratch_shapes=[
                pltpu.VMEM((2 * CHIPS, BINS, 2 * heads, WIDTH, HEAD), BF16),
                pltpu.SemaphoreType.DMA((2 * CHIPS, BINS)),
            ],
        ),
        out_shape=out_shape,
        cost_estimate=pl.CostEstimate(flops=4 * pairs * HEAD, bytes_accessed=heads * (4 << 20), transcendentals=pairs),
        compiler_params=pltpu.CompilerParams(vmem_limit_bytes=48 << 20),
        name=name,
    )(scalars, q, *kv)


def forward_kernel(sizes, at, bin_of, r_ref, *refs):
    u_ref, r_buf, u_buf, in_sem, out_sems = refs[-5:]
    arrive = pltpu.make_async_copy(r_ref.at[:, pl.ds(0, r_buf.shape[1])], r_buf, in_sem)
    arrive.start()
    arrive.wait()

    def leave(row):
        return pltpu.make_async_copy(u_buf.at[row], u_ref.at[row, pl.ds(at, u_buf.shape[1])], out_sems.at[row])

    for row in range(ROWS):
        for slot in range(BINS):
            b = bin_of[row * BINS + slot]
            base = 0
            for size in sizes:
                for n in range(size):
                    u_buf[row, base + slot * size + n] = r_buf[b // BINS, base + (b % BINS) * size + n]
                base += BINS * size
        leave(row).start()
    for row in range(ROWS):
        leave(row).wait()


def forward(bin_of, received, sizes, into, name):
    hbm = pl.BlockSpec(memory_space=pltpu.HBM)
    count = BINS * sum(sizes)
    at = 0 if into is None else into.shape[1] - count
    return pl.pallas_call(
        functools.partial(forward_kernel, sizes, at),
        grid_spec=pltpu.PrefetchScalarGridSpec(
            num_scalar_prefetch=1,
            grid=(),
            in_specs=[pl.BlockSpec(memory_space=pl.ANY)] + [hbm] * (0 if into is None else 1),
            out_specs=hbm,
            scratch_shapes=[
                pltpu.VMEM((ROWS, count, PIECE, HEAD), BF16),
                pltpu.VMEM((ROWS, count, PIECE, HEAD), BF16),
                pltpu.SemaphoreType.DMA,
                pltpu.SemaphoreType.DMA((ROWS,)),
            ],
        ),
        out_shape=blocks(count) if into is None else jax.ShapeDtypeStruct(into.shape, BF16),
        input_output_aliases={} if into is None else {2: 0},
        cost_estimate=pl.CostEstimate(flops=0, bytes_accessed=4 << 20, transcendentals=0),
        name=name,
    )(bin_of, received, *(() if into is None else (into,)))


def place_kernel(at, heads, column, r_ref, _, out_ref, r_buf, out_buf, in_sems, out_sems):
    size = HALF * heads

    def arrive(slot):
        return pltpu.make_async_copy(r_ref.at[:, pl.ds(at + slot * size, size)], r_buf.at[slot], in_sems.at[slot])

    def leave(slot):
        columns = pl.ds(column, heads * GROUP * HEAD)
        return pltpu.make_async_copy(out_buf.at[slot], out_ref.at[slot, 0, :, columns], out_sems.at[slot])

    for slot in range(BINS):
        arrive(slot).start()
    for slot in range(BINS):
        arrive(slot).wait()
        for j in range(ROWS):
            for n in range(size):
                head = (n // HALF) * GROUP + (j % 2) * HALF + n % HALF
                out_buf[slot, pl.ds((j // 2) * PIECE, PIECE), pl.ds(head * HEAD, HEAD)] = r_buf[slot, j, n]
        leave(slot).start()
    for slot in range(BINS):
        leave(slot).wait()


def place(received, at, heads, out, column, name):
    hbm = pl.BlockSpec(memory_space=pltpu.HBM)
    return pl.pallas_call(
        functools.partial(place_kernel, at, heads, column),
        in_specs=[pl.BlockSpec(memory_space=pl.ANY), hbm],
        out_specs=hbm,
        out_shape=jax.ShapeDtypeStruct(out.shape, out.dtype),
        scratch_shapes=[
            pltpu.VMEM((BINS, ROWS, HALF * heads, PIECE, HEAD), BF16),
            pltpu.VMEM((BINS, WIDTH, heads * GROUP * HEAD), BF16),
            pltpu.SemaphoreType.DMA((BINS,)),
            pltpu.SemaphoreType.DMA((BINS,)),
        ],
        input_output_aliases={1: 0},
        cost_estimate=pl.CostEstimate(flops=0, bytes_accessed=heads * (2 << 20), transcendentals=0),
        name=name,
    )(received, out)


def fetch(kv):
    pieces = [kv]
    for back in range(1, CHIPS):
        pairs = [(2 * x + core, 2 * (x + back) + core) for x in range(CHIPS - back) for core in range(2)]
        pieces.append(lax.ppermute(kv, "ctx", pairs))
    return pieces


def share(pieces):
    swap = [(c, c ^ 1) for c in range(2 * CHIPS)]
    return [p for piece in pieces for p in (piece, lax.ppermute(piece, "ctx", swap))]


def exchange(sent):
    return lax.all_to_all(sent, "dp", split_axis=0, concat_axis=0, tiled=True)


def shards(queries, key_rows, bin_value_rows, lengths, routes):
    my_row = lax.axis_index("dp")
    ctx = lax.axis_index("ctx").astype(jnp.int32)
    flat = routes[:, 0]
    order = jnp.arange(ROWS * BINS, dtype=jnp.int32)
    earlier = (flat[:, None] == flat[None, :]) & (order[None, :] < order[:, None])
    slot = flat * BINS + jnp.sum(earlier.astype(jnp.int32), axis=1)
    bin_of = jnp.sum(jnp.where(slot[None, :] == order[:, None], order[None, :], 0), axis=1).astype(jnp.int32)
    flat_lengths = lengths.reshape(-1)

    def key_value(heads):
        columns = [slice(h * HEAD, (h + 1) * HEAD) for h in heads]
        return jnp.stack([a[:, 0, :, c] for c in columns for a in (key_rows, bin_value_rows)])

    def query_spec(first):
        return pl.BlockSpec((1, 1, WIDTH, GROUP * HEAD), lambda b, h, s: (b, 0, 0, first + h))

    def piece_spec(first, heads):
        return pl.BlockSpec((ROWS, HALF, PIECE, HEAD), lambda b, h, s: (0, first + b * heads + h, 0, 0))

    near_a = fetch(key_value([1]))
    pieces_a = share(near_a)
    got_1 = exchange(pack(flat_lengths, queries, key_rows, bin_value_rows))

    kv_b, near_a[3] = lax.optimization_barrier((key_value([2, 3]), near_a[3]))
    near_b = fetch(kv_b)

    here = jnp.concatenate([flat_lengths, ctx[None]])
    second = attend(here, queries, pieces_a, 1, query_spec(1), piece_spec(0, 1), blocks(36), False, True, "attend_a")
    second = forward(bin_of, got_1, (HALF, 1), second, "forward_q")
    second, near_b = lax.optimization_barrier((second, near_b))
    got_2 = exchange(second)

    digits = got_1[:, 5 * BINS, 0, : 6 * BINS].astype(jnp.float32).astype(jnp.int32)
    all_lengths = (digits[:, : 3 * BINS] * 32 + digits[:, 3 * BINS :]).reshape(ROWS * BINS, 3)
    my_bins = lax.dynamic_slice_in_dim(bin_of, my_row * BINS, BINS)
    slot_lengths = jnp.sum(jnp.where(my_bins[:, None, None] == order[None, :, None], all_lengths[None], 0), axis=1)
    there = jnp.concatenate([slot_lengths.reshape(-1).astype(jnp.int32), ctx[None]])

    pieces_b = share(near_b)
    third = attend(here, queries, pieces_b, 2, query_spec(2), piece_spec(0, 2), blocks(48), False, True, "attend_b")
    third = forward(bin_of, got_2, (HALF,), third, "forward_a")
    third, there = lax.optimization_barrier((third, there))
    got_3 = exchange(third)

    kv_0 = jnp.transpose(got_2[:, 32:].reshape(PARTS, 2, BINS, PIECE, HEAD), (1, 2, 0, 3, 4))
    pieces_0 = share(fetch(kv_0.reshape(2, BINS, WIDTH, HEAD)))
    full = jax.ShapeDtypeStruct(queries.shape, BF16)
    out = attend(there, got_2, pieces_0, 1, piece_spec(4, 1), query_spec(0), full, True, False, "attend_0")

    fourth = forward(bin_of, got_3, (2 * HALF,), None, "forward_b")
    fourth, out = lax.optimization_barrier((fourth, out))
    got_4 = exchange(fourth)
    out = place(got_3, 32, 1, out, GROUP * HEAD, "place_a")
    return place(got_4, 0, 2, out, 2 * GROUP * HEAD, "place_b")


def solution(mesh):
    in_specs = (
        P("dp", "ctx", None, None),
        P("dp", "ctx", None, None),
        P("dp", "ctx", None, None),
        P("dp", None),
        P(),
    )
    out_specs = P("dp", "ctx", None, None)
    return jax.shard_map(shards, mesh=mesh, in_specs=in_specs, out_specs=out_specs, check_vma=False)
```

time: 549 us -> 191 us (0.35); the launches traced: 539 us -> 190 us
  waiting for transfers between devices: 269 us -> 86.7 us
  matrix products: 109 us -> 0 us
  local copies, waits for them, and re-layouts: 109 us -> 6.09 us
  Pallas kernels: 0 us -> 51.6 us
  between operations: 13.7 us -> 0.57 us
  starting transfers between devices: 34.3 us -> 43 us
    all_to_all x4, waiting for transfers between devices: 227 us -> 52.9 us  [exchange(): return lax.all_to_all(sent, 'dp', split_axis=0, concat_axis=0, tiled=True)]
    dot_general x8 -> x0, matrix products: 79.6 us -> none  [the longest x6 45.5 us: arrange(): jnp.einsum('sb,bcwf->scwf', table.astype(jnp.bfloat16), arrays, preferred...]
    pallas_call x0 -> x9, Pallas kernels: none -> 51.6 us  [the longest x3 34 us: attend(): pl.pallas_call(functools.partial(attend_kernel, from_pieces, to_pieces),...]
    reshape x10 -> x3, local copies, waits for them, and re-layouts: 43.6 us -> 1.38 us  [the longest x1 1.27 us: shards(): flat_lengths = lengths.reshape(-1)]
    all_gather x2 -> x0, waiting for transfers between devices: 41.9 us -> none  [the longest x1 24.5 us: shards(): lax.all_gather(slot_k, 'ctx', axis=1, tiled=True)]
    ppermute x0 -> x21, waiting for transfers between devices: none -> 33.8 us  [the longest x9 29.5 us: fetch(): pieces.append(lax.ppermute(kv, 'ctx', pairs))]
    sub x2 -> x0, matrix products: 29.5 us -> none  [one_block(): weights = jnp.where(seen_b, jnp.exp(scores - top), 0.0)]
    convert_element_type x4 -> x0, local copies, waits for them, and re-layouts: 23.6 us -> none  [the longest x3 23.5 us: arrange(): return jnp.einsum('sb,bcwf->scwf', table.astype(jnp.bfloat16), arrays, pr...]
  transfers between devices with their start and end apart: 6 -> 25, of which waited for: 5 -> 13; matrix products, arithmetic and copies ran while one was open for 11% -> 1% of each run, Pallas kernels for 0% -> 21%
where the time goes in v1:
time: 191 us; the launch traced here: 190 us
  waiting for transfers between devices  86.7 us (45%)
  Pallas kernels  51.6 us (27%)
  starting transfers between devices  43 us (23%)
  local copies, waits for them, and re-layouts  6.09 us (3%)
  other arithmetic  2.13 us (1%)
    all_to_all x4, waiting for transfers between devices, exchange(): return lax.all_to_all(sent, 'dp', split_axis=0, concat_axis=0, tiled=True)  52.9 us
    pallas_call x3, Pallas kernels, attend(): pl.pallas_call(functools.partial(attend_kernel, from_pieces, to_pieces),...  34 us
    ppermute x9, waiting for transfers between devices, fetch(): pieces.append(lax.ppermute(kv, 'ctx', pairs))  29.5 us
    all_to_all x4, starting transfers between devices, exchange(): return lax.all_to_all(sent, 'dp', split_axis=0, concat_axis=0, tiled=True)  24 us
    ppermute x9, starting transfers between devices, fetch(): pieces.append(lax.ppermute(kv, 'ctx', pairs))  16.2 us
    pallas_call x3, Pallas kernels, forward(): pl.pallas_call(functools.partial(forward_kernel, sizes, at), grid_spec=pl...  10.1 us
    pallas_call x2, Pallas kernels, place(): pl.pallas_call(functools.partial(place_kernel, at, heads, column), in_spe...  4.53 us
    ppermute x12, waiting for transfers between devices, share(): lax.ppermute(piece, 'ctx', swap)  4.28 us
  transfers between devices with their start and end apart: 25, of which 13 were waited for; matrix products, arithmetic and copies ran while one was open for 1% of the time, Pallas kernels for 21%

profile of v1, /device:TPU:4, one launch (start us, length us, event | category | flops | bytes accessed | tf_op | source)
XLA Modules:
  0.0 190.1 jit_solution(12750204118062898232)
XLA Ops:
  1.3 3.0 %pack.1 = bf16[16,21,16,128]{3,2,1,0:T(8,128)(2,1)} custom-call(s32[12]{0:T(128)} %reshape.49.lengths, bf16[4,1,128,4096]{3,2,1,0:T(8,128)(2,1)} %q_ref.5, bf16[4,1,128,512]{3,2,1,0:T(8,128)(2,1)} %k_ref.1, bf16[4,1,128,512]{3,2,1,0:T(8,128)(2,1)} %v_ref.1), custom_call_target="tpu_custom_call" | custom-call | bytes 4194304 | tf_op jit(solution)/shard_map/pack/pallas_call | solution.py:69
  4.3 8.2 %all-to-all-start = ((bf16[16,21,16,128]{3,2,1,0:T(8,128)(2,1)}), bf16[16,21,16,128]{3,2,1,0:T(8,128)(2,1)}, u32[]{:S(2)}, u32[]{:S(2)}) async-start(bf16[16,21,16,128]{3,2,1,0:T(8,128)(2,1)} %pack.1), calls=%async_computation | async-start | bytes 2752512 | tf_op jit(solution)/shard_map/all_to_all | solution.py:295
  14.8 3.7 %collective-permute-start.1 = (bf16[2,4,128,128]{3,2,1,0:T(8,128)(2,1)S(1)}, bf16[2,4,128,128]{3,2,1,0:T(8,128)(2,1)S(1)}, u32[]{:S(2)}, u32[]{:S(2)}) collective-permute-start(bf16[2,4,128,128]{3,2,1,0:T(8,128)(2,1)S(1)} %pad_maximum_fusion.1.refs_0_), channel_id=1, source_target_pairs={{0,2},{1,3},{2,4},{3,5},{4,6},{5,7},{8,10},{9,11},{10,12},{11,13},... | collective-permute-start | bytes 786440 | tf_op jit(solution)/shard_map/ppermute | solution.py:285
  20.1 6.5 %collective-permute-done.3.refs_4_ = bf16[2,4,128,128]{3,2,1,0:T(8,128)(2,1)S(1)} collective-permute-done((bf16[2,4,128,128]{3,2,1,0:T(8,128)(2,1)S(1)}, bf16[2,4,128,128]{3,2,1,0:T(8,128)(2,1)S(1)}, u32[]{:S(2)}, u32[]{:S(2)}) %collective-permute-start.3) | collective-permute-done | bytes 262176 | tf_op jit(solution)/shard_map/ppermute | solution.py:285
  27.8 2.8 %collective-permute-done.1.refs_2_ = bf16[2,4,128,128]{3,2,1,0:T(8,128)(2,1)S(1)} collective-permute-done((bf16[2,4,128,128]{3,2,1,0:T(8,128)(2,1)S(1)}, bf16[2,4,128,128]{3,2,1,0:T(8,128)(2,1)S(1)}, u32[]{:S(2)}, u32[]{:S(2)}) %collective-permute-start.1) | collective-permute-done | bytes 262176 | tf_op jit(solution)/shard_map/ppermute | solution.py:285
  30.6 4.6 %collective-permute-start.7 = (bf16[4,4,128,128]{3,2,1,0:T(8,128)(2,1)S(1)}, bf16[4,4,128,128]{3,2,1,0:T(8,128)(2,1)}, u32[]{:S(2)}, u32[]{:S(2)}) collective-permute-start(bf16[4,4,128,128]{3,2,1,0:T(8,128)(2,1)S(1)} %pad_maximum_fusion.refs_0_), channel_id=1, source_target_pairs={{0,2},{1,3},{2,4},{3,5},{4,6},{5,7},{8,10},{9,11},{10,12},{11,13},... | collective-permute-start | bytes 1572872 | tf_op jit(solution)/shard_map/ppermute | solution.py:285
  37.3 9.0 %attend_a.1.refs_0_ = bf16[16,36,16,128]{3,2,1,0:T(8,128)(2,1)S(1)} custom-call(s32[13]{0:T(128)S(1)} %pad_add_fusion.scalars, bf16[4,1,128,4096]{3,2,1,0:T(8,128)(2,1)} %q_ref.5, bf16[2,4,128,128]{3,2,1,0:T(8,128)(2,1)S(1)} %pad_maximum_fusion.1.refs_0_, bf16[2,4,128,128]{3,2,1,0:T(8,128)(2,1)S(1)} %collective-permute-done.refs_1_, ...), custom_call_target="tpu_custom_call" | custom-call | flops 2147483648 | bytes 4194304 | tf_op jit(solution)/shard_map/attend_a/pallas_call | solution.py:173
  47.7 3.2 %forward_q.1 = bf16[16,36,16,128]{3,2,1,0:T(8,128)(2,1)} custom-call(s32[64]{0:T(128)} %select_reduce_fusion.bin_of, bf16[16,21,16,128]{3,2,1,0:T(8,128)(2,1)} %all-to-all-done.r_ref, bf16[16,36,16,128]{3,2,1,0:T(8,128)(2,1)} %copy-done.2), custom_call_target="tpu_custom_call", output_to_operand_aliasing={{}: (2, {})} | custom-call | bytes 4194304 | tf_op jit(solution)/shard_map/forward_q/pallas_call | solution.py:218
  51.0 8.7 %collective-permute-done.7.refs_2_ = bf16[4,4,128,128]{3,2,1,0:T(8,128)(2,1)} collective-permute-done((bf16[4,4,128,128]{3,2,1,0:T(8,128)(2,1)S(1)}, bf16[4,4,128,128]{3,2,1,0:T(8,128)(2,1)}, u32[]{:S(2)}, u32[]{:S(2)}) %collective-permute-start.7) | collective-permute-done | bytes 524320 | tf_op jit(solution)/shard_map/ppermute | solution.py:285
  59.7 6.9 %all-to-all-start.1 = ((bf16[16,36,16,128]{3,2,1,0:T(8,128)(2,1)}), bf16[16,36,16,128]{3,2,1,0:T(8,128)(2,1)S(1)}, u32[]{:S(2)}, u32[]{:S(2)}) async-start(bf16[16,36,16,128]{3,2,1,0:T(8,128)(2,1)} %forward_q.1), calls=%async_computation.1 | async-start | bytes 4718592 | tf_op jit(solution)/shard_map/all_to_all | solution.py:295
  71.3 16.1 %attend_b.1.refs_0_ = bf16[16,48,16,128]{3,2,1,0:T(8,128)(2,1)} custom-call(s32[13]{0:T(128)S(1)} %pad_add_fusion.scalars, bf16[4,1,128,4096]{3,2,1,0:T(8,128)(2,1)} %q_ref.5, bf16[4,4,128,128]{3,2,1,0:T(8,128)(2,1)S(1)} %pad_maximum_fusion.refs_0_, bf16[4,4,128,128]{3,2,1,0:T(8,128)(2,1)} %collective-permute-done.10.refs_1_, ...), custom_call_target="tpu_custom_call" | custom-call | flops 4294967296 | bytes 8388608 | tf_op jit(solution)/shard_map/attend_b/pallas_call | solution.py:173
  87.4 13.2 %all-to-all-done.1.r_ref.q_ref = bf16[16,36,16,128]{3,2,1,0:T(8,128)(2,1)S(1)} async-done(((bf16[16,36,16,128]{3,2,1,0:T(8,128)(2,1)}), bf16[16,36,16,128]{3,2,1,0:T(8,128)(2,1)S(1)}, u32[]{:S(2)}, u32[]{:S(2)}) %all-to-all-start.1) | async-done | bytes 2359328 | tf_op jit(solution)/shard_map/all_to_all | solution.py:295
  102.0 3.1 %forward_a.1 = bf16[16,48,16,128]{3,2,1,0:T(8,128)(2,1)} custom-call(s32[64]{0:T(128)} %select_reduce_fusion.bin_of, bf16[16,36,16,128]{3,2,1,0:T(8,128)(2,1)} %copy-done, bf16[16,48,16,128]{3,2,1,0:T(8,128)(2,1)} %attend_b.1.refs_0_), custom_call_target="tpu_custom_call", output_to_operand_aliasing={{}: (2, {})} | custom-call | bytes 4194304 | tf_op jit(solution)/shard_map/forward_a/pallas_call | solution.py:218
  105.1 4.9 %all-to-all-start.2 = ((bf16[16,48,16,128]{3,2,1,0:T(8,128)(2,1)}), bf16[16,48,16,128]{3,2,1,0:T(8,128)(2,1)}, u32[]{:S(2)}, u32[]{:S(2)}) async-start(bf16[16,48,16,128]{3,2,1,0:T(8,128)(2,1)} %forward_a.1), calls=%async_computation.2 | async-start | bytes 6291456 | tf_op jit(solution)/shard_map/all_to_all | solution.py:295
  112.0 1.9 %collective-permute-start.15 = (bf16[2,4,128,128]{3,2,1,0:T(8,128)(2,1)S(1)}, bf16[2,4,128,128]{3,2,1,0:T(8,128)(2,1)S(1)}, u32[]{:S(2)}, u32[]{:S(2)}) collective-permute-start(bf16[2,4,128,128]{3,2,1,0:T(8,128)(2,1)S(1)} %bitcast.25), channel_id=1, source_target_pairs={{0,2},{1,3},{2,4},{3,5},{4,6},{5,7},{8,10},{9,11},{10,12},{11,13},... | collective-permute-start | bytes 786440 | tf_op jit(solution)/shard_map/ppermute | solution.py:285
  114.5 8.8 %collective-permute-done.17.refs_4_ = bf16[2,4,128,128]{3,2,1,0:T(8,128)(2,1)S(1)} collective-permute-done((bf16[2,4,128,128]{3,2,1,0:T(8,128)(2,1)S(1)}, bf16[2,4,128,128]{3,2,1,0:T(8,128)(2,1)S(1)}, u32[]{:S(2)}, u32[]{:S(2)}) %collective-permute-start.17) | collective-permute-done | bytes 262176 | tf_op jit(solution)/shard_map/ppermute | solution.py:285
  123.4 2.8 %collective-permute-done.15.refs_2_ = bf16[2,4,128,128]{3,2,1,0:T(8,128)(2,1)S(1)} collective-permute-done((bf16[2,4,128,128]{3,2,1,0:T(8,128)(2,1)S(1)}, bf16[2,4,128,128]{3,2,1,0:T(8,128)(2,1)S(1)}, u32[]{:S(2)}, u32[]{:S(2)}) %collective-permute-start.15) | collective-permute-done | bytes 262176 | tf_op jit(solution)/shard_map/ppermute | solution.py:285
  127.7 8.8 %attend_0.1._ = bf16[4,1,128,4096]{3,2,1,0:T(8,128)(2,1)} custom-call(s32[13]{0:T(128)S(1)} %pad_add_fusion.1.scalars, bf16[16,36,16,128]{3,2,1,0:T(8,128)(2,1)S(1)} %copy-done.1, bf16[2,4,128,128]{3,2,1,0:T(8,128)(2,1)S(1)} %bitcast.27, bf16[2,4,128,128]{3,2,1,0:T(8,128)(2,1)S(1)} %collective-permute-done.14.refs_1_, ...), custom_call_target="tpu_custom_call" | custom-call | flops 2147483648 | bytes 4194304 | tf_op jit(solution)/shard_map/attend_0/pallas_call | solution.py:173
  136.5 15.0 %all-to-all-done.2.r_ref = bf16[16,48,16,128]{3,2,1,0:T(8,128)(2,1)} async-done(((bf16[16,48,16,128]{3,2,1,0:T(8,128)(2,1)}), bf16[16,48,16,128]{3,2,1,0:T(8,128)(2,1)}, u32[]{:S(2)}, u32[]{:S(2)}) %all-to-all-start.2) | async-done | bytes 3145760 | tf_op jit(solution)/shard_map/all_to_all | solution.py:295
  151.5 3.8 %forward_b.1 = bf16[16,32,16,128]{3,2,1,0:T(8,128)(2,1)} custom-call(s32[64]{0:T(128)} %select_reduce_fusion.bin_of, bf16[16,48,16,128]{3,2,1,0:T(8,128)(2,1)} %all-to-all-done.2.r_ref), custom_call_target="tpu_custom_call" | custom-call | bytes 4194304 | tf_op jit(solution)/shard_map/forward_b/pallas_call | solution.py:218
  155.3 4.0 %all-to-all-start.3 = ((bf16[16,32,16,128]{3,2,1,0:T(8,128)(2,1)}), bf16[16,32,16,128]{3,2,1,0:T(8,128)(2,1)S(1)}, u32[]{:S(2)}, u32[]{:S(2)}) async-start(bf16[16,32,16,128]{3,2,1,0:T(8,128)(2,1)} %forward_b.1), calls=%async_computation.3 | async-start | bytes 4194304 | tf_op jit(solution)/shard_map/all_to_all | solution.py:295
  159.3 2.0 %place_a.1._ = bf16[4,1,128,4096]{3,2,1,0:T(8,128)(2,1)} custom-call(bf16[16,48,16,128]{3,2,1,0:T(8,128)(2,1)} %all-to-all-done.2.r_ref, bf16[4,1,128,4096]{3,2,1,0:T(8,128)(2,1)} %attend_0.1._), custom_call_target="tpu_custom_call", output_to_operand_aliasing={{}: (1, {})} | custom-call | bytes 2097152 | tf_op jit(solution)/shard_map/place_a/pallas_call | solution.py:264
  161.3 24.7 %all-to-all-done.3.r_ref = bf16[16,32,16,128]{3,2,1,0:T(8,128)(2,1)S(1)} async-done(((bf16[16,32,16,128]{3,2,1,0:T(8,128)(2,1)}), bf16[16,32,16,128]{3,2,1,0:T(8,128)(2,1)S(1)}, u32[]{:S(2)}, u32[]{:S(2)}) %all-to-all-start.3) | async-done | bytes 2097184 | tf_op jit(solution)/shard_map/all_to_all | solution.py:295
  187.4 2.5 %place_b.1 = bf16[4,1,128,4096]{3,2,1,0:T(8,128)(2,1)} custom-call(bf16[16,32,16,128]{3,2,1,0:T(8,128)(2,1)} %copy-done.3, bf16[4,1,128,4096]{3,2,1,0:T(8,128)(2,1)} %place_a.1._), custom_call_target="tpu_custom_call", output_to_operand_aliasing={{}: (1, {})} | custom-call | bytes 4194304 | tf_op jit(solution)/shard_map/place_b/pallas_call | solution.py:264
  (74 shorter events, 21.2 us)
Async XLA Ops:
  4.3 43.4 %all-to-all-start = ((bf16[16,21,16,128]{3,2,1,0:T(8,128)(2,1)}), bf16[16,21,16,128]{3,2,1,0:T(8,128)(2,1)}, u32[]{:S(2)}, u32[]{:S(2)}) async-start(bf16[16,21,16,128]{3,2,1,0:T(8,128)(2,1)} %pack.1), calls=%async_computation | async-start | bytes 2752512 | tf_op jit(solution)/shard_map/all_to_all | solution.py:295
  12.8 5.8 %collective-permute-start.5 = (bf16[2,4,128,128]{3,2,1,0:T(8,128)(2,1)S(1)}, bf16[2,4,128,128]{3,2,1,0:T(8,128)(2,1)S(1)}, u32[]{:S(2)}, u32[]{:S(2)}) collective-permute-start(bf16[2,4,128,128]{3,2,1,0:T(8,128)(2,1)S(1)} %pad_maximum_fusion.1.refs_0_), channel_id=1, source_target_pairs={{0,6},{1,7},{8,14},{9,15},{16,22},{17,23},{24,30},{25,31},{32,38},... | collective-permute-start | bytes 786440 | tf_op jit(solution)/shard_map/ppermute | solution.py:285
  13.5 13.0 %collective-permute-start.3 = (bf16[2,4,128,128]{3,2,1,0:T(8,128)(2,1)S(1)}, bf16[2,4,128,128]{3,2,1,0:T(8,128)(2,1)S(1)}, u32[]{:S(2)}, u32[]{:S(2)}) collective-permute-start(bf16[2,4,128,128]{3,2,1,0:T(8,128)(2,1)S(1)} %pad_maximum_fusion.1.refs_0_), channel_id=1, source_target_pairs={{0,4},{1,5},{2,6},{3,7},{8,12},{9,13},{10,14},{11,15},{16,20},{17,... | collective-permute-start | bytes 786440 | tf_op jit(solution)/shard_map/ppermute | solution.py:285
  14.8 15.8 %collective-permute-start.1 = (bf16[2,4,128,128]{3,2,1,0:T(8,128)(2,1)S(1)}, bf16[2,4,128,128]{3,2,1,0:T(8,128)(2,1)S(1)}, u32[]{:S(2)}, u32[]{:S(2)}) collective-permute-start(bf16[2,4,128,128]{3,2,1,0:T(8,128)(2,1)S(1)} %pad_maximum_fusion.1.refs_0_), channel_id=1, source_target_pairs={{0,2},{1,3},{2,4},{3,5},{4,6},{5,7},{8,10},{9,11},{10,12},{11,13},... | collective-permute-start | bytes 786440 | tf_op jit(solution)/shard_map/ppermute | solution.py:285
  18.5 16.8 %collective-permute-start = (bf16[2,4,128,128]{3,2,1,0:T(8,128)(2,1)S(1)}, bf16[2,4,128,128]{3,2,1,0:T(8,128)(2,1)S(1)}, u32[]{:S(2)}, u32[]{:S(2)}) collective-permute-start(bf16[2,4,128,128]{3,2,1,0:T(8,128)(2,1)S(1)} %pad_maximum_fusion.1.refs_0_), channel_id=1, source_target_pairs={{0,1},{1,0},{2,3},{3,2},{4,5},{5,4},{6,7},{7,6},{8,9},{9,8},{10,11... | collective-permute-start | bytes 786440 | tf_op jit(solution)/shard_map/ppermute | solution.py:291
  18.6 17.0 %collective-permute-start.6 = (bf16[2,4,128,128]{3,2,1,0:T(8,128)(2,1)S(1)}, bf16[2,4,128,128]{3,2,1,0:T(8,128)(2,1)S(1)}, u32[]{:S(2)}, u32[]{:S(2)}) collective-permute-start(bf16[2,4,128,128]{3,2,1,0:T(8,128)(2,1)S(1)} %collective-permute-done.5.refs_6_), channel_id=1, source_target_pairs={{0,1},{1,0},{2,3},{3,2},{4,5},{5,4},{6,7},{7,6},{8,9},{9,8},{10,11... | collective-permute-start | bytes 786440 | tf_op jit(solution)/shard_map/ppermute | solution.py:291
  19.4 31.6 %collective-permute-start.9 = (bf16[4,4,128,128]{3,2,1,0:T(8,128)(2,1)S(1)}, bf16[4,4,128,128]{3,2,1,0:T(8,128)(2,1)S(1)}, u32[]{:S(2)}, u32[]{:S(2)}) collective-permute-start(bf16[4,4,128,128]{3,2,1,0:T(8,128)(2,1)S(1)} %pad_maximum_fusion.refs_0_), channel_id=1, source_target_pairs={{0,6},{1,7},{8,14},{9,15},{16,22},{17,23},{24,30},{25,31},{32,38},... | collective-permute-start | bytes 1572872 | tf_op jit(solution)/shard_map/ppermute | solution.py:285
  26.5 24.5 %collective-permute-start.8 = (bf16[4,4,128,128]{3,2,1,0:T(8,128)(2,1)S(1)}, bf16[4,4,128,128]{3,2,1,0:T(8,128)(2,1)}, u32[]{:S(2)}, u32[]{:S(2)}) collective-permute-start(bf16[4,4,128,128]{3,2,1,0:T(8,128)(2,1)S(1)} %pad_maximum_fusion.refs_0_), channel_id=1, source_target_pairs={{0,4},{1,5},{2,6},{3,7},{8,12},{9,13},{10,14},{11,15},{16,20},{17,... | collective-permute-start | bytes 1572872 | tf_op jit(solution)/shard_map/ppermute | solution.py:285
  30.6 29.1 %collective-permute-start.7 = (bf16[4,4,128,128]{3,2,1,0:T(8,128)(2,1)S(1)}, bf16[4,4,128,128]{3,2,1,0:T(8,128)(2,1)}, u32[]{:S(2)}, u32[]{:S(2)}) collective-permute-start(bf16[4,4,128,128]{3,2,1,0:T(8,128)(2,1)S(1)} %pad_maximum_fusion.refs_0_), channel_id=1, source_target_pairs={{0,2},{1,3},{2,4},{3,5},{4,6},{5,7},{8,10},{9,11},{10,12},{11,13},... | collective-permute-start | bytes 1572872 | tf_op jit(solution)/shard_map/ppermute | solution.py:285
  35.3 1.6 collective-permute-start.4
  35.6 1.7 collective-permute-start.2
  59.7 40.9 %all-to-all-start.1 = ((bf16[16,36,16,128]{3,2,1,0:T(8,128)(2,1)}), bf16[16,36,16,128]{3,2,1,0:T(8,128)(2,1)S(1)}, u32[]{:S(2)}, u32[]{:S(2)}) async-start(bf16[16,36,16,128]{3,2,1,0:T(8,128)(2,1)} %forward_q.1), calls=%async_computation.1 | async-start | bytes 4718592 | tf_op jit(solution)/shard_map/all_to_all | solution.py:295
  66.8 2.4 %collective-permute-start.10 = (bf16[4,4,128,128]{3,2,1,0:T(8,128)(2,1)S(1)}, bf16[4,4,128,128]{3,2,1,0:T(8,128)(2,1)}, u32[]{:S(2)}, u32[]{:S(2)}) collective-permute-start(bf16[4,4,128,128]{3,2,1,0:T(8,128)(2,1)S(1)} %pad_maximum_fusion.refs_0_), channel_id=1, source_target_pairs={{0,1},{1,0},{2,3},{3,2},{4,5},{5,4},{6,7},{7,6},{8,9},{9,8},{10,11... | collective-permute-start | bytes 1572872 | tf_op jit(solution)/shard_map/ppermute | solution.py:291
  66.8 3.5 %collective-permute-start.11 = (bf16[4,4,128,128]{3,2,1,0:T(8,128)(2,1)}, bf16[4,4,128,128]{3,2,1,0:T(8,128)(2,1)}, u32[]{:S(2)}, u32[]{:S(2)}) collective-permute-start(bf16[4,4,128,128]{3,2,1,0:T(8,128)(2,1)} %collective-permute-done.7.refs_2_), channel_id=1, source_target_pairs={{0,1},{1,0},{2,3},{3,2},{4,5},{5,4},{6,7},{7,6},{8,9},{9,8},{10,11... | collective-permute-start | bytes 1572872 | tf_op jit(solution)/shard_map/ppermute | solution.py:291
  67.3 4.0 %collective-permute-start.12 = (bf16[4,4,128,128]{3,2,1,0:T(8,128)(2,1)}, bf16[4,4,128,128]{3,2,1,0:T(8,128)(2,1)}, u32[]{:S(2)}, u32[]{:S(2)}) collective-permute-start(bf16[4,4,128,128]{3,2,1,0:T(8,128)(2,1)} %collective-permute-done.8.refs_4_), channel_id=1, source_target_pairs={{0,1},{1,0},{2,3},{3,2},{4,5},{5,4},{6,7},{7,6},{8,9},{9,8},{10,11... | collective-permute-start | bytes 1572872 | tf_op jit(solution)/shard_map/ppermute | solution.py:291
  67.3 3.9 %collective-permute-start.13 = (bf16[4,4,128,128]{3,2,1,0:T(8,128)(2,1)S(1)}, bf16[4,4,128,128]{3,2,1,0:T(8,128)(2,1)}, u32[]{:S(2)}, u32[]{:S(2)}) collective-permute-start(bf16[4,4,128,128]{3,2,1,0:T(8,128)(2,1)S(1)} %collective-permute-done.9.refs_6_), channel_id=1, source_target_pairs={{0,1},{1,0},{2,3},{3,2},{4,5},{5,4},{6,7},{7,6},{8,9},{9,8},{10,11... | collective-permute-start | bytes 1572872 | tf_op jit(solution)/shard_map/ppermute | solution.py:291
  105.1 46.4 %all-to-all-start.2 = ((bf16[16,48,16,128]{3,2,1,0:T(8,128)(2,1)}), bf16[16,48,16,128]{3,2,1,0:T(8,128)(2,1)}, u32[]{:S(2)}, u32[]{:S(2)}) async-start(bf16[16,48,16,128]{3,2,1,0:T(8,128)(2,1)} %forward_a.1), calls=%async_computation.2 | async-start | bytes 6291456 | tf_op jit(solution)/shard_map/all_to_all | solution.py:295
  110.0 4.0 %collective-permute-start.19 = (bf16[2,4,128,128]{3,2,1,0:T(8,128)(2,1)S(1)}, bf16[2,4,128,128]{3,2,1,0:T(8,128)(2,1)S(1)}, u32[]{:S(2)}, u32[]{:S(2)}) collective-permute-start(bf16[2,4,128,128]{3,2,1,0:T(8,128)(2,1)S(1)} %bitcast.23), channel_id=1, source_target_pairs={{0,6},{1,7},{8,14},{9,15},{16,22},{17,23},{24,30},{25,31},{32,38},... | collective-permute-start | bytes 786440 | tf_op jit(solution)/shard_map/ppermute | solution.py:285
  110.7 12.6 %collective-permute-start.17 = (bf16[2,4,128,128]{3,2,1,0:T(8,128)(2,1)S(1)}, bf16[2,4,128,128]{3,2,1,0:T(8,128)(2,1)S(1)}, u32[]{:S(2)}, u32[]{:S(2)}) collective-permute-start(bf16[2,4,128,128]{3,2,1,0:T(8,128)(2,1)S(1)} %bitcast.24), channel_id=1, source_target_pairs={{0,4},{1,5},{2,6},{3,7},{8,12},{9,13},{10,14},{11,15},{16,20},{17,... | collective-permute-start | bytes 786440 | tf_op jit(solution)/shard_map/ppermute | solution.py:285
  112.0 14.1 %collective-permute-start.15 = (bf16[2,4,128,128]{3,2,1,0:T(8,128)(2,1)S(1)}, bf16[2,4,128,128]{3,2,1,0:T(8,128)(2,1)S(1)}, u32[]{:S(2)}, u32[]{:S(2)}) collective-permute-start(bf16[2,4,128,128]{3,2,1,0:T(8,128)(2,1)S(1)} %bitcast.25), channel_id=1, source_target_pairs={{0,2},{1,3},{2,4},{3,5},{4,6},{5,7},{8,10},{9,11},{10,12},{11,13},... | collective-permute-start | bytes 786440 | tf_op jit(solution)/shard_map/ppermute | solution.py:285
  113.9 12.2 %collective-permute-start.14 = (bf16[2,4,128,128]{3,2,1,0:T(8,128)(2,1)S(1)}, bf16[2,4,128,128]{3,2,1,0:T(8,128)(2,1)S(1)}, u32[]{:S(2)}, u32[]{:S(2)}) collective-permute-start(bf16[2,4,128,128]{3,2,1,0:T(8,128)(2,1)S(1)} %bitcast.26), channel_id=1, source_target_pairs={{0,1},{1,0},{2,3},{3,2},{4,5},{5,4},{6,7},{7,6},{8,9},{9,8},{10,11... | collective-permute-start | bytes 786440 | tf_op jit(solution)/shard_map/ppermute | solution.py:291
  114.1 12.1 %collective-permute-start.20 = (bf16[2,4,128,128]{3,2,1,0:T(8,128)(2,1)S(1)}, bf16[2,4,128,128]{3,2,1,0:T(8,128)(2,1)S(1)}, u32[]{:S(2)}, u32[]{:S(2)}) collective-permute-start(bf16[2,4,128,128]{3,2,1,0:T(8,128)(2,1)S(1)} %collective-permute-done.19.refs_6_), channel_id=1, source_target_pairs={{0,1},{1,0},{2,3},{3,2},{4,5},{5,4},{6,7},{7,6},{8,9},{9,8},{10,11... | collective-permute-start | bytes 786440 | tf_op jit(solution)/shard_map/ppermute | solution.py:291
  123.4 2.8 %collective-permute-start.18 = (bf16[2,4,128,128]{3,2,1,0:T(8,128)(2,1)S(1)}, bf16[2,4,128,128]{3,2,1,0:T(8,128)(2,1)S(1)}, u32[]{:S(2)}, u32[]{:S(2)}) collective-permute-start(bf16[2,4,128,128]{3,2,1,0:T(8,128)(2,1)S(1)} %collective-permute-done.17.refs_4_), channel_id=1, source_target_pairs={{0,1},{1,0},{2,3},{3,2},{4,5},{5,4},{6,7},{7,6},{8,9},{9,8},{10,11... | collective-permute-start | bytes 786440 | tf_op jit(solution)/shard_map/ppermute | solution.py:291
  155.3 30.8 %all-to-all-start.3 = ((bf16[16,32,16,128]{3,2,1,0:T(8,128)(2,1)}), bf16[16,32,16,128]{3,2,1,0:T(8,128)(2,1)S(1)}, u32[]{:S(2)}, u32[]{:S(2)}) async-start(bf16[16,32,16,128]{3,2,1,0:T(8,128)(2,1)} %forward_b.1), calls=%async_computation.3 | async-start | bytes 4194304 | tf_op jit(solution)/shard_map/all_to_all | solution.py:295
  (11 other events, 111.9 us)

commit v2 on v1

v2 whole, which is shorter than its diff:
```python
import functools
import math

import jax
import jax.numpy as jnp
from jax import lax
from jax.experimental import pallas as pl
from jax.experimental.pallas import tpu as pltpu
from jax.sharding import PartitionSpec as P

BINS = 4
ROWS = 16
CHIPS = 4
WIDTH = 128
HEAD = 128
GROUP = 8
PIECE = 16
PARTS = WIDTH // PIECE
HALF = GROUP // 2
NEG = -1e30
BF16 = jnp.bfloat16
VMEM_LIMIT = 40 << 20


def blocks(count):
    return pltpu.HBM((ROWS, count, PIECE, HEAD), BF16)


def pack_kernel(lengths, q_ref, k_ref, v_ref, u_ref, q_buf, k_buf, v_buf, u_buf, in_sems, out_sems):
    def arrive(b):
        wide, narrow = pl.ds(0, GROUP * HEAD), pl.ds(0, HEAD)
        return [
            pltpu.make_async_copy(q_ref.at[b, 0, :, wide], q_buf.at[b], in_sems.at[0, b]),
            pltpu.make_async_copy(k_ref.at[b, 0, :, narrow], k_buf.at[b], in_sems.at[1, b]),
            pltpu.make_async_copy(v_ref.at[b, 0, :, narrow], v_buf.at[b], in_sems.at[2, b]),
        ]

    def leave(i):
        part = pl.ds(i * HALF, HALF if i < BINS else BINS + 1)
        return pltpu.make_async_copy(u_buf.at[:, part], u_ref.at[:, part], out_sems.at[i])

    for b in range(BINS):
        for copy in arrive(b):
            copy.start()
    lane = lax.broadcasted_iota(jnp.int32, (PIECE, HEAD), 1)
    digits = jnp.zeros((PIECE, HEAD), jnp.int32)
    for i in range(3 * BINS):
        length = lengths[i // 3, i % 3]
        digits = jnp.where(lane == i, length // 32, digits)
        digits = jnp.where(lane == 3 * BINS + i, length % 32, digits)
    digits = digits.astype(jnp.float32).astype(BF16)
    for b in range(BINS):
        for copy in arrive(b):
            copy.wait()
        for j in range(ROWS):
            rows = pl.ds((j // 2) * PIECE, PIECE)
            for n in range(HALF):
                u_buf[j, b * HALF + n] = q_buf[b, rows, pl.ds(((j % 2) * HALF + n) * HEAD, HEAD)]
            u_buf[j, BINS * HALF + b] = (k_buf if j % 2 == 0 else v_buf)[b, rows]
            if b == 0:
                u_buf[j, BINS * HALF + BINS] = digits
        leave(b).start()
    leave(BINS).start()
    for i in range(BINS + 1):
        leave(i).wait()


def pack(lengths, queries, key_rows, value_rows):
    hbm = pl.BlockSpec(memory_space=pltpu.HBM)
    count = BINS * HALF + BINS + 1
    return pl.pallas_call(
        pack_kernel,
        grid_spec=pltpu.PrefetchScalarGridSpec(
            num_scalar_prefetch=1,
            grid=(),
            in_specs=[hbm] * 3,
            out_specs=hbm,
            scratch_shapes=[
                pltpu.VMEM((BINS, WIDTH, GROUP * HEAD), BF16),
                pltpu.VMEM((BINS, WIDTH, HEAD), BF16),
                pltpu.VMEM((BINS, WIDTH, HEAD), BF16),
                pltpu.VMEM((ROWS, count, PIECE, HEAD), BF16),
                pltpu.SemaphoreType.DMA((3, BINS)),
                pltpu.SemaphoreType.DMA((BINS + 1,)),
            ],
        ),
        out_shape=blocks(count),
        cost_estimate=pl.CostEstimate(flops=0, bytes_accessed=4 << 20, transcendentals=0),
        compiler_params=pltpu.CompilerParams(vmem_limit_bytes=VMEM_LIMIT),
        name="pack",
    )(lengths, *(pltpu.with_memory_space_constraint(a, pltpu.HBM) for a in (queries, key_rows, value_rows)))


def attend_kernel(head_at, from_pieces, to_pieces, lengths, place, q_ref, *refs):
    kv_refs, (out_ref, buffer, sems) = refs[: 2 * CHIPS], refs[-3:]
    item = pl.program_id(0)
    ctx = place[0]
    chip, core = ctx // 2, ctx % 2
    prompt = lengths[item, 0]
    split = prompt + lengths[item, 1]
    end = split + lengths[item, 2]
    start = ctx * WIDTH
    factor = math.log2(math.e) / math.sqrt(HEAD)

    def copy(i, b):
        return pltpu.make_async_copy(kv_refs[i].at[pl.ds(2 * head_at, 2), b], buffer.at[i, b], sems.at[i, b])

    @pl.when(item == 0)
    def _():
        for b in range(BINS):
            for i in range(2 * CHIPS):

                @pl.when(i // 2 <= chip)
                def _(i=i, b=b):
                    copy(i, b).start()

    for i in range(2 * CHIPS):

        @pl.when(i // 2 <= chip)
        def _(i=i):
            copy(i, item).wait()

    def read_head(head):
        if not from_pieces:
            return q_ref[0, 0, :, pl.ds(head * HEAD, HEAD)]
        return jnp.concatenate([q_ref[2 * r + head // HALF, head % HALF] for r in range(PARTS)], axis=0)

    def write_head(head, rows):
        if to_pieces:
            for r in range(PARTS):
                out_ref[2 * r + head // HALF, head % HALF] = rows[r * PIECE : (r + 1) * PIECE]
        else:
            out_ref[0, 0, :, pl.ds(head * HEAD, HEAD)] = rows

    def attend(chips):
        keys = jnp.concatenate([buffer[i, item, 0] for i in range(2 * chips)], axis=0)
        values = jnp.concatenate([buffer[i, item, 1] for i in range(2 * chips)], axis=0)
        t = start + lax.broadcasted_iota(jnp.int32, (WIDTH, WIDTH), 0)
        biases = []
        for i in range(2 * chips):
            origin = 2 * (chip - i // 2) + (core if i % 2 == 0 else 1 - core)
            u = origin * WIDTH + lax.broadcasted_iota(jnp.int32, (WIDTH, WIDTH), 1)
            hidden = (u > t) | ((t >= split) & (u >= prompt) & (u < split))
            biases.append(jnp.where(hidden, NEG, 0.0))
        bias = jnp.concatenate(biases, axis=1)
        live = (start + lax.broadcasted_iota(jnp.int32, (WIDTH, 1), 0)) < end
        bias = jnp.concatenate([bias, bias], axis=0)
        live = jnp.concatenate([live, live], axis=0)
        n = GROUP // 2
        qs = [jnp.concatenate([read_head(2 * i), read_head(2 * i + 1)], axis=0) for i in range(n)]
        scores = [lax.dot_general(q, keys, (((1,), (1,)), ((), ())), preferred_element_type=jnp.float32) + bias for q in qs]
        tops = [jnp.max(x, axis=1, keepdims=True) for x in scores]
        weights = [jnp.exp2((x - top) * factor) for x, top in zip(scores, tops)]
        wide = jnp.concatenate([values, jnp.ones_like(values)], axis=1)
        mixed = [jnp.dot(x.astype(BF16), wide, preferred_element_type=jnp.float32) for x in weights]
        for i in range(n):
            out = (mixed[i][:, :HEAD] * jnp.where(live, 1.0 / mixed[i][:, HEAD:], 0.0)).astype(BF16)
            write_head(2 * i, out[:WIDTH])
            write_head(2 * i + 1, out[WIDTH:])

    @pl.when(end <= start)
    def _():
        out_ref[...] = jnp.zeros_like(out_ref)

    for chips in range(1, CHIPS + 1):

        @pl.when((end > start) & (chip == chips - 1))
        def _(chips=chips):
            attend(chips)


def attend(lengths, place, q, kv, q_spec, out_spec, out_shape, name, from_pieces=False, to_pieces=True, into=None, head_at=0, weight=1):
    hbm = pl.BlockSpec(memory_space=pltpu.HBM)
    pairs = BINS * GROUP * WIDTH * WIDTH * 2 * CHIPS
    return pl.pallas_call(
        functools.partial(attend_kernel, head_at, from_pieces, to_pieces),
        grid_spec=pltpu.PrefetchScalarGridSpec(
            num_scalar_prefetch=2,
            grid=(BINS,),
            in_specs=[q_spec] + [hbm] * (2 * CHIPS + (0 if into is None else 1)),
            out_specs=out_spec,
            scratch_shapes=[
                pltpu.VMEM((2 * CHIPS, BINS, 2, WIDTH, HEAD), BF16),
                pltpu.SemaphoreType.DMA((2 * CHIPS, BINS)),
            ],
        ),
        out_shape=out_shape,
        input_output_aliases={} if into is None else {3 + 2 * CHIPS: 0},
        cost_estimate=pl.CostEstimate(flops=int(weight * 20 * pairs * HEAD), bytes_accessed=4 << 20, transcendentals=pairs),
        compiler_params=pltpu.CompilerParams(vmem_limit_bytes=VMEM_LIMIT),
        name=name,
    )(lengths, place, *(pltpu.with_memory_space_constraint(a, pltpu.HBM) for a in (q, *kv)), *(() if into is None else (into,)))


def forward_kernel(sizes, at, bin_of, r_ref, *refs):
    u_ref, u_buf, sems = refs[-3:]

    def leave(row):
        return pltpu.make_async_copy(u_buf.at[row], u_ref.at[row, pl.ds(at, u_buf.shape[1])], sems.at[row])

    for row in range(ROWS):
        for slot in range(BINS):
            b = bin_of[row * BINS + slot]
            base = 0
            for size in sizes:
                for n in range(size):
                    u_buf[row, base + slot * size + n] = r_ref[b // BINS, base + (b % BINS) * size + n]
                base += BINS * size
        leave(row).start()
    for row in range(ROWS):
        leave(row).wait()


def forward(bin_of, received, sizes, into, name):
    hbm = pl.BlockSpec(memory_space=pltpu.HBM)
    count = BINS * sum(sizes)
    at = 0 if into is None else into.shape[1] - count
    return pl.pallas_call(
        functools.partial(forward_kernel, sizes, at),
        grid_spec=pltpu.PrefetchScalarGridSpec(
            num_scalar_prefetch=1,
            grid=(),
            in_specs=[pl.BlockSpec(memory_space=pltpu.VMEM)] + [hbm] * (0 if into is None else 1),
            out_specs=hbm,
            scratch_shapes=[pltpu.VMEM((ROWS, count, PIECE, HEAD), BF16), pltpu.SemaphoreType.DMA((ROWS,))],
        ),
        out_shape=blocks(count) if into is None else blocks(into.shape[1]),
        input_output_aliases={} if into is None else {2: 0},
        cost_estimate=pl.CostEstimate(flops=0, bytes_accessed=4 << 20, transcendentals=0),
        compiler_params=pltpu.CompilerParams(vmem_limit_bytes=VMEM_LIMIT),
        name=name,
    )(bin_of, pltpu.with_memory_space_constraint(received, pltpu.VMEM), *(() if into is None else (into,)))


def place_kernel(at, column, r_ref, _, out_ref, out_buf, sems):
    heads = len(at)

    def leave(slot):
        columns = pl.ds(column, heads * GROUP * HEAD)
        return pltpu.make_async_copy(out_buf.at[slot], out_ref.at[slot, 0, :, columns], sems.at[slot])

    for slot in range(BINS):
        for j in range(ROWS):
            for n in range(HALF * heads):
                head = (n // HALF) * GROUP + (j % 2) * HALF + n % HALF
                rows, columns = pl.ds((j // 2) * PIECE, PIECE), pl.ds(head * HEAD, HEAD)
                out_buf[slot, rows, columns] = r_ref[j, at[n // HALF] + slot * HALF + n % HALF]
        leave(slot).start()
    for slot in range(BINS):
        leave(slot).wait()


def place(received, at, out, column, name):
    hbm = pl.BlockSpec(memory_space=pltpu.HBM)
    heads = len(at)
    return pl.pallas_call(
        functools.partial(place_kernel, at, column),
        in_specs=[pl.BlockSpec(memory_space=pltpu.VMEM), hbm],
        out_specs=hbm,
        out_shape=jax.ShapeDtypeStruct(out.shape, out.dtype),
        scratch_shapes=[
            pltpu.VMEM((BINS, WIDTH, heads * GROUP * HEAD), BF16),
            pltpu.SemaphoreType.DMA((BINS,)),
        ],
        input_output_aliases={1: 0},
        cost_estimate=pl.CostEstimate(flops=0, bytes_accessed=heads * (2 << 20), transcendentals=0),
        compiler_params=pltpu.CompilerParams(vmem_limit_bytes=VMEM_LIMIT),
        name=name,
    )(pltpu.with_memory_space_constraint(received, pltpu.VMEM), out)


def fetch(kv):
    pieces = [kv]
    for back in range(1, CHIPS):
        pairs = [(c, (c + 2 * back) % (2 * CHIPS)) for c in range(2 * CHIPS)]
        pieces.append(lax.ppermute(kv, "ctx", pairs))
    return pieces


def share(pieces):
    swap = [(c, c ^ 1) for c in range(2 * CHIPS)]
    return [p for piece in pieces for p in (piece, lax.ppermute(piece, "ctx", swap))]


def exchange(sent):
    return lax.all_to_all(sent, "dp", split_axis=0, concat_axis=0, tiled=True)


def shards(queries, key_rows, bin_value_rows, lengths, routes):
    my_row = lax.axis_index("dp")
    ctx = lax.axis_index("ctx").astype(jnp.int32)[None]
    flat = routes[:, 0]
    order = jnp.arange(ROWS * BINS, dtype=jnp.int32)
    earlier = (flat[:, None] == flat[None, :]) & (order[None, :] < order[:, None])
    slot = flat * BINS + jnp.sum(earlier.astype(jnp.int32), axis=1)
    bin_of = jnp.sum(jnp.where(slot[None, :] == order[:, None], order[None, :], 0), axis=1).astype(jnp.int32)

    def key_value(heads, near=None):
        k, v = key_rows, bin_value_rows
        if near is not None:
            k, v, near[CHIPS - 1] = lax.optimization_barrier((k, v, near[CHIPS - 1]))
        columns = [slice(head * HEAD, (head + 1) * HEAD) for head in heads]
        return jnp.stack([a[:, 0, :, c] for c in columns for a in (k, v)])

    def query_spec(head):
        return pl.BlockSpec((1, 1, WIDTH, GROUP * HEAD), lambda b, *_: (b, 0, 0, head))

    def piece_spec(group):
        return pl.BlockSpec((ROWS, HALF, PIECE, HEAD), lambda b, *_: (0, group * BINS + b, 0, 0))

    near_1 = fetch(key_value([1]))
    got_1 = exchange(pack(lengths, queries, key_rows, bin_value_rows))
    near_23 = fetch(key_value([2, 3], near_1))

    second = attend(lengths, ctx, queries, share(near_1), query_spec(1), piece_spec(0), blocks(36), "attend_1")
    second = forward(bin_of, got_1, (HALF, 1), second, "forward_0")
    got_2 = exchange(second)
    near_23[1:], _ = lax.optimization_barrier((near_23[1:], second))

    digits = got_1[:, 5 * BINS, 0, : 6 * BINS].astype(jnp.float32).astype(jnp.int32)
    all_lengths = (digits[:, : 3 * BINS] * 32 + digits[:, 3 * BINS :]).reshape(ROWS * BINS, 3)
    my_bins = lax.dynamic_slice_in_dim(bin_of, my_row * BINS, BINS)
    slot_lengths = jnp.sum(jnp.where(my_bins[:, None, None] == order[None, :, None], all_lengths[None], 0), axis=1).astype(jnp.int32)

    pieces_23 = share(near_23)
    third = attend(lengths, ctx, queries, pieces_23, query_spec(2), piece_spec(0), blocks(48), "attend_2", weight=3)
    third = attend(lengths, ctx, queries, pieces_23, query_spec(3), piece_spec(1), blocks(48), "attend_3", into=third, head_at=1, weight=3)
    third = forward(bin_of, got_2, (HALF,), third, "forward_1")
    third, slot_lengths = lax.optimization_barrier((third, slot_lengths))
    got_3 = exchange(third)

    kv_0 = jnp.transpose(got_2[:, 32:].reshape(PARTS, 2, BINS, PIECE, HEAD), (1, 2, 0, 3, 4))
    pieces_0 = share(fetch(kv_0.reshape(2, BINS, WIDTH, HEAD)))
    full = jax.ShapeDtypeStruct(queries.shape, BF16)
    out = attend(slot_lengths, ctx, got_2, pieces_0, piece_spec(1), query_spec(0), full, "attend_0", True, False)

    fourth = forward(bin_of, got_3, (HALF, HALF), None, "forward_23")
    fourth, out = lax.optimization_barrier((fourth, out))
    got_4 = exchange(fourth)
    out = place(got_3, (32,), out, GROUP * HEAD, "place_1")
    return place(got_4, (0, 16), out, 2 * GROUP * HEAD, "place_23")


def solution(mesh):
    in_specs = (
        P("dp", "ctx", None, None),
        P("dp", "ctx", None, None),
        P("dp", "ctx", None, None),
        P("dp", None),
        P(),
    )
    out_specs = P("dp", "ctx", None, None)
    return jax.shard_map(shards, mesh=mesh, in_specs=in_specs, out_specs=out_specs, check_vma=False)
```

time: 191 us -> 163 us (0.85)
  waiting for transfers between devices: 86.7 us -> 66.6 us
  starting transfers between devices: 43 us -> 35.8 us
  local copies, waits for them, and re-layouts: 6.09 us -> 3.89 us
    ppermute x9, waiting for transfers between devices: 29.5 us -> 10 us  [fetch(): pieces.append(lax.ppermute(kv, 'ctx', pairs))]
    pallas_call x5 -> x6, Pallas kernels: 38.5 us -> 43.2 us  [the longest x4 39.2 us: attend(): pl.pallas_call(functools.partial(attend_kernel, head_at, from_pieces, to_...]
    pallas_call x3, Pallas kernels: 10.1 us -> 5.74 us  [forward(): pl.pallas_call(functools.partial(forward_kernel, sizes, at), grid_spec=pl...]
    ppermute x9, starting transfers between devices: 16.2 us -> 12.7 us  [fetch(): pieces.append(lax.ppermute(kv, 'ctx', pairs))]
    unnamed x18 -> x28, local copies, waits for them, and re-layouts: 4.2 us -> 1.5 us
    all_to_all x4, starting transfers between devices: 24 us -> 21.7 us  [exchange(): return lax.all_to_all(sent, 'dp', split_axis=0, concat_axis=0, tiled=True)]
  transfers between devices with their start and end apart: 25 -> 25, of which waited for: 13 -> 13; matrix products, arithmetic and copies ran while one was open for 1% -> 2% of each run, Pallas kernels for 21% -> 28%
where the time goes in v2:
time: 163 us; the launch traced here: 160 us
  waiting for transfers between devices  66.6 us (41%)
  Pallas kernels  51.9 us (32%)
  starting transfers between devices  35.8 us (22%)
  local copies, waits for them, and re-layouts  3.89 us (2%)
    all_to_all x4, waiting for transfers between devices, exchange(): return lax.all_to_all(sent, 'dp', split_axis=0, concat_axis=0, tiled=True)  52.7 us
    pallas_call x4, Pallas kernels, attend(): pl.pallas_call(functools.partial(attend_kernel, head_at, from_pieces, to_...  39.2 us
    all_to_all x4, starting transfers between devices, exchange(): return lax.all_to_all(sent, 'dp', split_axis=0, concat_axis=0, tiled=True)  21.7 us
    ppermute x9, starting transfers between devices, fetch(): pieces.append(lax.ppermute(kv, 'ctx', pairs))  12.7 us
    ppermute x9, waiting for transfers between devices, fetch(): pieces.append(lax.ppermute(kv, 'ctx', pairs))  10 us
    pallas_call x3, Pallas kernels, forward(): pl.pallas_call(functools.partial(forward_kernel, sizes, at), grid_spec=pl...  5.74 us
    pallas_call x2, Pallas kernels, place(): pl.pallas_call(functools.partial(place_kernel, at, column), in_specs=[pl....  4.07 us
    ppermute x12, waiting for transfers between devices, share(): lax.ppermute(piece, 'ctx', swap)  3.87 us
  transfers between devices with their start and end apart: 25, of which 13 were waited for; matrix products, arithmetic and copies ran while one was open for 2% of the time, Pallas kernels for 28%

profile of v2, /device:TPU:4, one launch (start us, length us, event | category | flops | bytes accessed | tf_op | source)
XLA Modules:
  0.0 160.2 jit_solution(6253712370945628284)
XLA Ops:
  1.7 1.5 collective-permute-start.1
  5.1 2.9 %pack.1 = bf16[16,21,16,128]{3,2,1,0:T(8,128)(2,1)} custom-call(s32[4,3]{1,0:T(4,128)S(1)} %copy-done.2, bf16[4,1,128,4096]{3,2,1,0:T(8,128)(2,1)} %q_ref.7, bf16[4,1,128,512]{3,2,1,0:T(8,128)(2,1)} %k_ref.1, bf16[4,1,128,512]{3,2,1,0:T(8,128)(2,1)} %v_ref.1), custom_call_target="tpu_custom_call" | custom-call | bytes 4194304 | tf_op jit(solution)/shard_map/pack/pallas_call | solution.py:71
  8.1 8.2 %all-to-all-start = ((bf16[16,21,16,128]{3,2,1,0:T(8,128)(2,1)}), bf16[16,21,16,128]{3,2,1,0:T(8,128)(2,1)S(1)}, u32[]{:S(2)}, u32[]{:S(2)}) async-start(bf16[16,21,16,128]{3,2,1,0:T(8,128)(2,1)} %pack.1), calls=%async_computation | async-start | bytes 2752512 | tf_op jit(solution)/shard_map/all_to_all | solution.py:286
  17.8 2.7 %collective-permute-start.10 = (bf16[4,4,128,128]{3,2,1,0:T(8,128)(2,1)S(1)}, bf16[4,4,128,128]{3,2,1,0:T(8,128)(2,1)}, u32[]{:S(2)}, u32[]{:S(2)}) collective-permute-start(bf16[4,4,128,128]{3,2,1,0:T(8,128)(2,1)S(1)} %pad_maximum_fusion.refs_0_), channel_id=1, source_target_pairs={{0,6},{1,7},{2,0},{3,1},{4,2},{5,3},{6,4},{7,5},{8,14},{9,15},{10,... | collective-permute-start | bytes 1572872 | tf_op jit(solution)/shard_map/ppermute | solution.py:276
  20.5 1.7 %collective-permute-start.9 = (bf16[4,4,128,128]{3,2,1,0:T(8,128)(2,1)S(1)}, bf16[4,4,128,128]{3,2,1,0:T(8,128)(2,1)}, u32[]{:S(2)}, u32[]{:S(2)}) collective-permute-start(bf16[4,4,128,128]{3,2,1,0:T(8,128)(2,1)S(1)} %pad_maximum_fusion.refs_0_), channel_id=1, source_target_pairs={{0,4},{1,5},{2,6},{3,7},{4,0},{5,1},{6,2},{7,3},{8,12},{9,13},{10,... | collective-permute-start | bytes 1572872 | tf_op jit(solution)/shard_map/ppermute | solution.py:276
  23.0 9.8 %attend_1.1.refs_0_ = bf16[16,36,16,128]{3,2,1,0:T(8,128)(2,1)} custom-call(s32[4,3]{1,0:T(4,128)S(1)} %copy-done.3, s32[1]{0:T(128)} %bitcast.1.place, bf16[4,1,128,4096]{3,2,1,0:T(8,128)(2,1)} %q_ref.7, bf16[2,4,128,128]{3,2,1,0:T(8,128)(2,1)} %copy-done.7, bf16[2,4,128,128]{3,2,1,0:T(8,128)(2,1)} %collective-permute-done.refs_1_, ...), custom_call_target="tpu_custom_call" | custom-call | flops 10737418240 | bytes 4194304 | tf_op jit(solution)/shard_map/attend_1/pallas_call | solution.py:175
  32.8 6.0 %all-to-all-done.r_ref = bf16[16,21,16,128]{3,2,1,0:T(8,128)(2,1)S(1)} async-done(((bf16[16,21,16,128]{3,2,1,0:T(8,128)(2,1)}), bf16[16,21,16,128]{3,2,1,0:T(8,128)(2,1)S(1)}, u32[]{:S(2)}, u32[]{:S(2)}) %all-to-all-start) | async-done | bytes 1376288 | tf_op jit(solution)/shard_map/all_to_all | solution.py:286
  38.8 1.8 %forward_0.1 = bf16[16,36,16,128]{3,2,1,0:T(8,128)(2,1)} custom-call(s32[64]{0:T(128)S(1)} %select_reduce_fusion.bin_of, bf16[16,21,16,128]{3,2,1,0:T(8,128)(2,1)S(1)} %all-to-all-done.r_ref, bf16[16,36,16,128]{3,2,1,0:T(8,128)(2,1)} %attend_1.1.refs_0_), custom_call_target="tpu_custom_call", output_to_operand_aliasing={{}: (2, {})} | custom-call | bytes 4194304 | tf_op jit(solution)/shard_map/forward_0/pallas_call | solution.py:218
  40.7 3.7 %all-to-all-start.1 = ((bf16[16,36,16,128]{3,2,1,0:T(8,128)(2,1)}), bf16[16,36,16,128]{3,2,1,0:T(8,128)(2,1)S(1)}, u32[]{:S(2)}, u32[]{:S(2)}) async-start(bf16[16,36,16,128]{3,2,1,0:T(8,128)(2,1)} %forward_0.1), calls=%async_computation.1 | async-start | bytes 4718592 | tf_op jit(solution)/shard_map/all_to_all | solution.py:286
  49.4 9.8 %attend_2.1.refs_8_ = bf16[16,48,16,128]{3,2,1,0:T(8,128)(2,1)} custom-call(s32[4,3]{1,0:T(4,128)S(1)} %copy-done.3, s32[1]{0:T(128)} %bitcast.1.place, bf16[4,1,128,4096]{3,2,1,0:T(8,128)(2,1)} %q_ref.7, bf16[4,4,128,128]{3,2,1,0:T(8,128)(2,1)} %copy-done.6, bf16[4,4,128,128]{3,2,1,0:T(8,128)(2,1)} %collective-permute-done.7.refs_1_, ...), custom_call_target="tpu_custom_call" | custom-call | flops 32212254720 | bytes 4194304 | tf_op jit(solution)/shard_map/attend_2/pallas_call | solution.py:175
  59.3 9.8 %attend_3.1.refs_0_ = bf16[16,48,16,128]{3,2,1,0:T(8,128)(2,1)} custom-call(s32[4,3]{1,0:T(4,128)S(1)} %copy-done.3, s32[1]{0:T(128)} %bitcast.1.place, bf16[4,1,128,4096]{3,2,1,0:T(8,128)(2,1)} %q_ref.7, bf16[4,4,128,128]{3,2,1,0:T(8,128)(2,1)} %copy-done.6, ...), custom_call_target="tpu_custom_call", output_to_operand_aliasing={{}: (11, {})} | custom-call | flops 32212254720 | bytes 4194304 | tf_op jit(solution)/shard_map/attend_3/pallas_call | solution.py:175
  69.1 8.1 %all-to-all-done.1.r_ref.q_ref = bf16[16,36,16,128]{3,2,1,0:T(8,128)(2,1)S(1)} async-done(((bf16[16,36,16,128]{3,2,1,0:T(8,128)(2,1)}), bf16[16,36,16,128]{3,2,1,0:T(8,128)(2,1)S(1)}, u32[]{:S(2)}, u32[]{:S(2)}) %all-to-all-start.1) | async-done | bytes 2359328 | tf_op jit(solution)/shard_map/all_to_all | solution.py:286
  77.2 1.8 %forward_1.1 = bf16[16,48,16,128]{3,2,1,0:T(8,128)(2,1)} custom-call(s32[64]{0:T(128)S(1)} %select_reduce_fusion.bin_of, bf16[16,36,16,128]{3,2,1,0:T(8,128)(2,1)S(1)} %all-to-all-done.1.r_ref.q_ref, bf16[16,48,16,128]{3,2,1,0:T(8,128)(2,1)} %attend_3.1.refs_0_), custom_call_target="tpu_custom_call", output_to_operand_aliasing={{}: (2, {})} | custom-call | bytes 4194304 | tf_op jit(solution)/shard_map/forward_1/pallas_call | solution.py:218
  79.1 3.9 %all-to-all-start.2 = ((bf16[16,48,16,128]{3,2,1,0:T(8,128)(2,1)}), bf16[16,48,16,128]{3,2,1,0:T(8,128)(2,1)S(1)}, u32[]{:S(2)}, u32[]{:S(2)}) async-start(bf16[16,48,16,128]{3,2,1,0:T(8,128)(2,1)} %forward_1.1), calls=%async_computation.2 | async-start | bytes 6291456 | tf_op jit(solution)/shard_map/all_to_all | solution.py:286
  84.0 1.4 collective-permute-start.15
  85.4 2.7 %collective-permute-start.17 = (bf16[2,4,128,128]{3,2,1,0:T(8,128)(2,1)S(1)}, bf16[2,4,128,128]{3,2,1,0:T(8,128)(2,1)}, u32[]{:S(2)}, u32[]{:S(2)}) collective-permute-start(bf16[2,4,128,128]{3,2,1,0:T(8,128)(2,1)S(1)} %bitcast.30), channel_id=1, source_target_pairs={{0,4},{1,5},{2,6},{3,7},{4,0},{5,1},{6,2},{7,3},{8,12},{9,13},{10,... | collective-permute-start | bytes 786440 | tf_op jit(solution)/shard_map/ppermute | solution.py:276
  89.0 5.0 %collective-permute-done.15.refs_2_ = bf16[2,4,128,128]{3,2,1,0:T(8,128)(2,1)} collective-permute-done((bf16[2,4,128,128]{3,2,1,0:T(8,128)(2,1)S(1)}, bf16[2,4,128,128]{3,2,1,0:T(8,128)(2,1)}, u32[]{:S(2)}, u32[]{:S(2)}) %collective-permute-start.15) | collective-permute-done | bytes 262176 | tf_op jit(solution)/shard_map/ppermute | solution.py:276
  93.9 3.1 %collective-permute-done.17.refs_4_ = bf16[2,4,128,128]{3,2,1,0:T(8,128)(2,1)} collective-permute-done((bf16[2,4,128,128]{3,2,1,0:T(8,128)(2,1)S(1)}, bf16[2,4,128,128]{3,2,1,0:T(8,128)(2,1)}, u32[]{:S(2)}, u32[]{:S(2)}) %collective-permute-start.17) | collective-permute-done | bytes 262176 | tf_op jit(solution)/shard_map/ppermute | solution.py:276
  99.6 9.7 %attend_0.1._ = bf16[4,1,128,4096]{3,2,1,0:T(8,128)(2,1)} custom-call(s32[4,3]{1,0:T(4,128)S(1)} %copy.33.lengths, s32[1]{0:T(128)} %bitcast.1.place, bf16[16,36,16,128]{3,2,1,0:T(8,128)(2,1)} %copy-done, bf16[2,4,128,128]{3,2,1,0:T(8,128)(2,1)} %bitcast.33, bf16[2,4,128,128]{3,2,1,0:T(8,128)(2,1)} %collective-permute-done.14.refs_1_, ...), custom_call_target="tpu_custom_call" | custom-call | flops 10737418240 | bytes 4194304 | tf_op jit(solution)/shard_map/attend_0/pallas_call | solution.py:175
  109.4 12.4 %all-to-all-done.2.r_ref = bf16[16,48,16,128]{3,2,1,0:T(8,128)(2,1)S(1)} async-done(((bf16[16,48,16,128]{3,2,1,0:T(8,128)(2,1)}), bf16[16,48,16,128]{3,2,1,0:T(8,128)(2,1)S(1)}, u32[]{:S(2)}, u32[]{:S(2)}) %all-to-all-start.2) | async-done | bytes 3145760 | tf_op jit(solution)/shard_map/all_to_all | solution.py:286
  121.7 2.1 %forward_23.1 = bf16[16,32,16,128]{3,2,1,0:T(8,128)(2,1)} custom-call(s32[64]{0:T(128)S(1)} %select_reduce_fusion.bin_of, bf16[16,48,16,128]{3,2,1,0:T(8,128)(2,1)S(1)} %all-to-all-done.2.r_ref), custom_call_target="tpu_custom_call" | custom-call | bytes 4194304 | tf_op jit(solution)/shard_map/forward_23/pallas_call | solution.py:218
  123.8 5.9 %all-to-all-start.3 = ((bf16[16,32,16,128]{3,2,1,0:T(8,128)(2,1)}), bf16[16,32,16,128]{3,2,1,0:T(8,128)(2,1)}, u32[]{:S(2)}, u32[]{:S(2)}) async-start(bf16[16,32,16,128]{3,2,1,0:T(8,128)(2,1)} %forward_23.1), calls=%async_computation.3 | async-start | bytes 4194304 | tf_op jit(solution)/shard_map/all_to_all | solution.py:286
  130.8 26.2 %all-to-all-done.3.r_ref = bf16[16,32,16,128]{3,2,1,0:T(8,128)(2,1)} async-done(((bf16[16,32,16,128]{3,2,1,0:T(8,128)(2,1)}), bf16[16,32,16,128]{3,2,1,0:T(8,128)(2,1)}, u32[]{:S(2)}, u32[]{:S(2)}) %all-to-all-start.3) | async-done | bytes 2097184 | tf_op jit(solution)/shard_map/all_to_all | solution.py:286
  157.0 3.0 %place_23.1 = bf16[4,1,128,4096]{3,2,1,0:T(8,128)(2,1)} custom-call(bf16[16,32,16,128]{3,2,1,0:T(8,128)(2,1)} %all-to-all-done.3.r_ref, bf16[4,1,128,4096]{3,2,1,0:T(8,128)(2,1)} %place_1.1._), custom_call_target="tpu_custom_call", output_to_operand_aliasing={{}: (1, {})} | custom-call | bytes 4194304 | tf_op jit(solution)/shard_map/place_23/pallas_call | solution.py:256
  (82 shorter events, 16.3 us)
Async XLA Ops:
  1.1 15.7 %collective-permute-start.5 = (bf16[2,4,128,128]{3,2,1,0:T(8,128)(2,1)S(1)}, bf16[2,4,128,128]{3,2,1,0:T(8,128)(2,1)S(1)}, u32[]{:S(2)}, u32[]{:S(2)}) collective-permute-start(bf16[2,4,128,128]{3,2,1,0:T(8,128)(2,1)S(1)} %pad_maximum_fusion.1.refs_0_), channel_id=1, source_target_pairs={{0,6},{1,7},{2,0},{3,1},{4,2},{5,3},{6,4},{7,5},{8,14},{9,15},{10,... | collective-permute-start | bytes 786440 | tf_op jit(solution)/shard_map/ppermute | solution.py:276
  1.7 15.3 %collective-permute-start.1 = (bf16[2,4,128,128]{3,2,1,0:T(8,128)(2,1)S(1)}, bf16[2,4,128,128]{3,2,1,0:T(8,128)(2,1)}, u32[]{:S(2)}, u32[]{:S(2)}) collective-permute-start(bf16[2,4,128,128]{3,2,1,0:T(8,128)(2,1)S(1)} %pad_maximum_fusion.1.refs_0_), channel_id=1, source_target_pairs={{0,2},{1,3},{2,4},{3,5},{4,6},{5,7},{6,0},{7,1},{8,10},{9,11},{10,... | collective-permute-start | bytes 786440 | tf_op jit(solution)/shard_map/ppermute | solution.py:276
  3.2 14.2 %collective-permute-start.3 = (bf16[2,4,128,128]{3,2,1,0:T(8,128)(2,1)S(1)}, bf16[2,4,128,128]{3,2,1,0:T(8,128)(2,1)}, u32[]{:S(2)}, u32[]{:S(2)}) collective-permute-start(bf16[2,4,128,128]{3,2,1,0:T(8,128)(2,1)S(1)} %pad_maximum_fusion.1.refs_0_), channel_id=1, source_target_pairs={{0,4},{1,5},{2,6},{3,7},{4,0},{5,1},{6,2},{7,3},{8,12},{9,13},{10,... | collective-permute-start | bytes 786440 | tf_op jit(solution)/shard_map/ppermute | solution.py:276
  4.4 16.1 %collective-permute-start = (bf16[2,4,128,128]{3,2,1,0:T(8,128)(2,1)S(1)}, bf16[2,4,128,128]{3,2,1,0:T(8,128)(2,1)}, u32[]{:S(2)}, u32[]{:S(2)}) collective-permute-start(bf16[2,4,128,128]{3,2,1,0:T(8,128)(2,1)S(1)} %pad_maximum_fusion.1.refs_0_), channel_id=1, source_target_pairs={{0,1},{1,0},{2,3},{3,2},{4,5},{5,4},{6,7},{7,6},{8,9},{9,8},{10,11... | collective-permute-start | bytes 786440 | tf_op jit(solution)/shard_map/ppermute | solution.py:282
  8.1 30.8 %all-to-all-start = ((bf16[16,21,16,128]{3,2,1,0:T(8,128)(2,1)}), bf16[16,21,16,128]{3,2,1,0:T(8,128)(2,1)S(1)}, u32[]{:S(2)}, u32[]{:S(2)}) async-start(bf16[16,21,16,128]{3,2,1,0:T(8,128)(2,1)} %pack.1), calls=%async_computation | async-start | bytes 2752512 | tf_op jit(solution)/shard_map/all_to_all | solution.py:286
  16.7 3.8 %collective-permute-start.6 = (bf16[2,4,128,128]{3,2,1,0:T(8,128)(2,1)S(1)}, bf16[2,4,128,128]{3,2,1,0:T(8,128)(2,1)S(1)}, u32[]{:S(2)}, u32[]{:S(2)}) collective-permute-start(bf16[2,4,128,128]{3,2,1,0:T(8,128)(2,1)S(1)} %collective-permute-done.5.refs_6_), channel_id=1, source_target_pairs={{0,1},{1,0},{2,3},{3,2},{4,5},{5,4},{6,7},{7,6},{8,9},{9,8},{10,11... | collective-permute-start | bytes 786440 | tf_op jit(solution)/shard_map/ppermute | solution.py:282
  17.0 5.2 %collective-permute-start.2 = (bf16[2,4,128,128]{3,2,1,0:T(8,128)(2,1)}, bf16[2,4,128,128]{3,2,1,0:T(8,128)(2,1)S(1)}, u32[]{:S(2)}, u32[]{:S(2)}) collective-permute-start(bf16[2,4,128,128]{3,2,1,0:T(8,128)(2,1)} %collective-permute-done.1.refs_2_), channel_id=1, source_target_pairs={{0,1},{1,0},{2,3},{3,2},{4,5},{5,4},{6,7},{7,6},{8,9},{9,8},{10,11... | collective-permute-start | bytes 786440 | tf_op jit(solution)/shard_map/ppermute | solution.py:282
  17.4 4.9 %collective-permute-start.4 = (bf16[2,4,128,128]{3,2,1,0:T(8,128)(2,1)}, bf16[2,4,128,128]{3,2,1,0:T(8,128)(2,1)S(1)}, u32[]{:S(2)}, u32[]{:S(2)}) collective-permute-start(bf16[2,4,128,128]{3,2,1,0:T(8,128)(2,1)} %collective-permute-done.3.refs_4_), channel_id=1, source_target_pairs={{0,1},{1,0},{2,3},{3,2},{4,5},{5,4},{6,7},{7,6},{8,9},{9,8},{10,11... | collective-permute-start | bytes 786440 | tf_op jit(solution)/shard_map/ppermute | solution.py:282
  17.8 26.6 %collective-permute-start.10 = (bf16[4,4,128,128]{3,2,1,0:T(8,128)(2,1)S(1)}, bf16[4,4,128,128]{3,2,1,0:T(8,128)(2,1)}, u32[]{:S(2)}, u32[]{:S(2)}) collective-permute-start(bf16[4,4,128,128]{3,2,1,0:T(8,128)(2,1)S(1)} %pad_maximum_fusion.refs_0_), channel_id=1, source_target_pairs={{0,6},{1,7},{2,0},{3,1},{4,2},{5,3},{6,4},{7,5},{8,14},{9,15},{10,... | collective-permute-start | bytes 1572872 | tf_op jit(solution)/shard_map/ppermute | solution.py:276
  20.5 25.2 %collective-permute-start.8 = (bf16[4,4,128,128]{3,2,1,0:T(8,128)(2,1)S(1)}, bf16[4,4,128,128]{3,2,1,0:T(8,128)(2,1)}, u32[]{:S(2)}, u32[]{:S(2)}) collective-permute-start(bf16[4,4,128,128]{3,2,1,0:T(8,128)(2,1)S(1)} %pad_maximum_fusion.refs_0_), channel_id=1, source_target_pairs={{0,2},{1,3},{2,4},{3,5},{4,6},{5,7},{6,0},{7,1},{8,10},{9,11},{10,... | collective-permute-start | bytes 1572872 | tf_op jit(solution)/shard_map/ppermute | solution.py:276
  20.5 25.2 %collective-permute-start.9 = (bf16[4,4,128,128]{3,2,1,0:T(8,128)(2,1)S(1)}, bf16[4,4,128,128]{3,2,1,0:T(8,128)(2,1)}, u32[]{:S(2)}, u32[]{:S(2)}) collective-permute-start(bf16[4,4,128,128]{3,2,1,0:T(8,128)(2,1)S(1)} %pad_maximum_fusion.refs_0_), channel_id=1, source_target_pairs={{0,4},{1,5},{2,6},{3,7},{4,0},{5,1},{6,2},{7,3},{8,12},{9,13},{10,... | collective-permute-start | bytes 1572872 | tf_op jit(solution)/shard_map/ppermute | solution.py:276
  22.2 25.2 %collective-permute-start.7 = (bf16[4,4,128,128]{3,2,1,0:T(8,128)(2,1)S(1)}, bf16[4,4,128,128]{3,2,1,0:T(8,128)(2,1)}, u32[]{:S(2)}, u32[]{:S(2)}) collective-permute-start(bf16[4,4,128,128]{3,2,1,0:T(8,128)(2,1)S(1)} %pad_maximum_fusion.refs_0_), channel_id=1, source_target_pairs={{0,1},{1,0},{2,3},{3,2},{4,5},{5,4},{6,7},{7,6},{8,9},{9,8},{10,11... | collective-permute-start | bytes 1572872 | tf_op jit(solution)/shard_map/ppermute | solution.py:282
  40.7 36.5 %all-to-all-start.1 = ((bf16[16,36,16,128]{3,2,1,0:T(8,128)(2,1)}), bf16[16,36,16,128]{3,2,1,0:T(8,128)(2,1)S(1)}, u32[]{:S(2)}, u32[]{:S(2)}) async-start(bf16[16,36,16,128]{3,2,1,0:T(8,128)(2,1)} %forward_0.1), calls=%async_computation.1 | async-start | bytes 4718592 | tf_op jit(solution)/shard_map/all_to_all | solution.py:286
  45.7 2.3 %collective-permute-start.11 = (bf16[4,4,128,128]{3,2,1,0:T(8,128)(2,1)}, bf16[4,4,128,128]{3,2,1,0:T(8,128)(2,1)}, u32[]{:S(2)}, u32[]{:S(2)}) collective-permute-start(bf16[4,4,128,128]{3,2,1,0:T(8,128)(2,1)} %collective-permute-done.8.refs_2_), channel_id=1, source_target_pairs={{0,1},{1,0},{2,3},{3,2},{4,5},{5,4},{6,7},{7,6},{8,9},{9,8},{10,11... | collective-permute-start | bytes 1572872 | tf_op jit(solution)/shard_map/ppermute | solution.py:282
  45.7 3.0 %collective-permute-start.12 = (bf16[4,4,128,128]{3,2,1,0:T(8,128)(2,1)}, bf16[4,4,128,128]{3,2,1,0:T(8,128)(2,1)}, u32[]{:S(2)}, u32[]{:S(2)}) collective-permute-start(bf16[4,4,128,128]{3,2,1,0:T(8,128)(2,1)} %collective-permute-done.9.refs_4_), channel_id=1, source_target_pairs={{0,1},{1,0},{2,3},{3,2},{4,5},{5,4},{6,7},{7,6},{8,9},{9,8},{10,11... | collective-permute-start | bytes 1572872 | tf_op jit(solution)/shard_map/ppermute | solution.py:282
  46.2 3.2 %collective-permute-start.13 = (bf16[4,4,128,128]{3,2,1,0:T(8,128)(2,1)}, bf16[4,4,128,128]{3,2,1,0:T(8,128)(2,1)}, u32[]{:S(2)}, u32[]{:S(2)}) collective-permute-start(bf16[4,4,128,128]{3,2,1,0:T(8,128)(2,1)} %collective-permute-done.10.refs_6_), channel_id=1, source_target_pairs={{0,1},{1,0},{2,3},{3,2},{4,5},{5,4},{6,7},{7,6},{8,9},{9,8},{10,11... | collective-permute-start | bytes 1572872 | tf_op jit(solution)/shard_map/ppermute | solution.py:282
  79.1 42.7 %all-to-all-start.2 = ((bf16[16,48,16,128]{3,2,1,0:T(8,128)(2,1)}), bf16[16,48,16,128]{3,2,1,0:T(8,128)(2,1)S(1)}, u32[]{:S(2)}, u32[]{:S(2)}) async-start(bf16[16,48,16,128]{3,2,1,0:T(8,128)(2,1)} %forward_1.1), calls=%async_computation.2 | async-start | bytes 6291456 | tf_op jit(solution)/shard_map/all_to_all | solution.py:286
  84.0 10.0 %collective-permute-start.15 = (bf16[2,4,128,128]{3,2,1,0:T(8,128)(2,1)S(1)}, bf16[2,4,128,128]{3,2,1,0:T(8,128)(2,1)}, u32[]{:S(2)}, u32[]{:S(2)}) collective-permute-start(bf16[2,4,128,128]{3,2,1,0:T(8,128)(2,1)S(1)} %bitcast.29), channel_id=1, source_target_pairs={{0,2},{1,3},{2,4},{3,5},{4,6},{5,7},{6,0},{7,1},{8,10},{9,11},{10,... | collective-permute-start | bytes 786440 | tf_op jit(solution)/shard_map/ppermute | solution.py:276
  85.4 11.6 %collective-permute-start.17 = (bf16[2,4,128,128]{3,2,1,0:T(8,128)(2,1)S(1)}, bf16[2,4,128,128]{3,2,1,0:T(8,128)(2,1)}, u32[]{:S(2)}, u32[]{:S(2)}) collective-permute-start(bf16[2,4,128,128]{3,2,1,0:T(8,128)(2,1)S(1)} %bitcast.30), channel_id=1, source_target_pairs={{0,4},{1,5},{2,6},{3,7},{4,0},{5,1},{6,2},{7,3},{8,12},{9,13},{10,... | collective-permute-start | bytes 786440 | tf_op jit(solution)/shard_map/ppermute | solution.py:276
  88.1 9.6 %collective-permute-start.19 = (bf16[2,4,128,128]{3,2,1,0:T(8,128)(2,1)S(1)}, bf16[2,4,128,128]{3,2,1,0:T(8,128)(2,1)}, u32[]{:S(2)}, u32[]{:S(2)}) collective-permute-start(bf16[2,4,128,128]{3,2,1,0:T(8,128)(2,1)S(1)} %bitcast.31), channel_id=1, source_target_pairs={{0,6},{1,7},{2,0},{3,1},{4,2},{5,3},{6,4},{7,5},{8,14},{9,15},{10,... | collective-permute-start | bytes 786440 | tf_op jit(solution)/shard_map/ppermute | solution.py:276
  89.0 8.9 %collective-permute-start.14 = (bf16[2,4,128,128]{3,2,1,0:T(8,128)(2,1)S(1)}, bf16[2,4,128,128]{3,2,1,0:T(8,128)(2,1)}, u32[]{:S(2)}, u32[]{:S(2)}) collective-permute-start(bf16[2,4,128,128]{3,2,1,0:T(8,128)(2,1)S(1)} %bitcast.32), channel_id=1, source_target_pairs={{0,1},{1,0},{2,3},{3,2},{4,5},{5,4},{6,7},{7,6},{8,9},{9,8},{10,11... | collective-permute-start | bytes 786440 | tf_op jit(solution)/shard_map/ppermute | solution.py:282
  93.9 3.9 %collective-permute-start.16 = (bf16[2,4,128,128]{3,2,1,0:T(8,128)(2,1)}, bf16[2,4,128,128]{3,2,1,0:T(8,128)(2,1)}, u32[]{:S(2)}, u32[]{:S(2)}) collective-permute-start(bf16[2,4,128,128]{3,2,1,0:T(8,128)(2,1)} %collective-permute-done.15.refs_2_), channel_id=1, source_target_pairs={{0,1},{1,0},{2,3},{3,2},{4,5},{5,4},{6,7},{7,6},{8,9},{9,8},{10,11... | collective-permute-start | bytes 786440 | tf_op jit(solution)/shard_map/ppermute | solution.py:282
  97.8 1.9 %collective-permute-start.20 = (bf16[2,4,128,128]{3,2,1,0:T(8,128)(2,1)}, bf16[2,4,128,128]{3,2,1,0:T(8,128)(2,1)}, u32[]{:S(2)}, u32[]{:S(2)}) collective-permute-start(bf16[2,4,128,128]{3,2,1,0:T(8,128)(2,1)} %collective-permute-done.19.refs_6_), channel_id=1, source_target_pairs={{0,1},{1,0},{2,3},{3,2},{4,5},{5,4},{6,7},{7,6},{8,9},{9,8},{10,11... | collective-permute-start | bytes 786440 | tf_op jit(solution)/shard_map/ppermute | solution.py:282
  123.8 33.2 %all-to-all-start.3 = ((bf16[16,32,16,128]{3,2,1,0:T(8,128)(2,1)}), bf16[16,32,16,128]{3,2,1,0:T(8,128)(2,1)}, u32[]{:S(2)}, u32[]{:S(2)}) async-start(bf16[16,32,16,128]{3,2,1,0:T(8,128)(2,1)} %forward_23.1), calls=%async_computation.3 | async-start | bytes 4194304 | tf_op jit(solution)/shard_map/all_to_all | solution.py:286
  (15 other events, 108.8 us)

commit v3 on v2

--- a/solution.py
+++ b/solution.py
@@ -88,12 +88,13 @@
         cost_estimate=pl.CostEstimate(flops=0, bytes_accessed=4 << 20, transcendentals=0),
         compiler_params=pltpu.CompilerParams(vmem_limit_bytes=VMEM_LIMIT),
         name="pack",
-    )(lengths, *(pltpu.with_memory_space_constraint(a, pltpu.HBM) for a in (queries, key_rows, value_rows)))
-
-
-def attend_kernel(head_at, from_pieces, to_pieces, lengths, place, q_ref, *refs):
-    kv_refs, (out_ref, buffer, sems) = refs[: 2 * CHIPS], refs[-3:]
-    item = pl.program_id(0)
+    )(*(pltpu.with_memory_space_constraint(a, pltpu.HBM) for a in (lengths, queries, key_rows, value_rows)))
+
+
+def attend_kernel(heads, part, q_at, out_at, from_pieces, to_pieces, lengths, place, q_ref, *refs):
+    kv_refs, (out_ref, buffer, q_buf, out_buf, sems, q_sems, out_sems) = refs[: 2 * CHIPS], refs[-7:]
+    step = pl.program_id(0)
+    item, head_at = step % BINS, step // BINS
     ctx = place[0]
     chip, core = ctx // 2, ctx % 2
     prompt = lengths[item, 0]
@@ -102,39 +103,71 @@
     start = ctx * WIDTH
     factor = math.log2(math.e) / math.sqrt(HEAD)
 
-    def copy(i, b):
-        return pltpu.make_async_copy(kv_refs[i].at[pl.ds(2 * head_at, 2), b], buffer.at[i, b], sems.at[i, b])
-
-    @pl.when(item == 0)
+    def active(w):
+        if part is None:
+            return True
+        late = (core == 0) & ((w // BINS == 1) | (chip < CHIPS // 2))
+        return late if part == "late" else jnp.logical_not(late)
+
+    def copy(i, w):
+        source = kv_refs[i].at[pl.ds(2 * (w // BINS), 2), w % BINS]
+        return pltpu.make_async_copy(source, buffer.at[i, w], sems.at[i, w])
+
+    def copy_q(w):
+        b, h = w % BINS, w // BINS
+        if from_pieces:
+            source = q_ref.at[:, pl.ds(q_at + w * HALF, HALF)]
+        else:
+            column = q_at + h * GROUP * HEAD
+            column = column if isinstance(column, int) else pl.multiple_of(column, GROUP * HEAD)
+            source = q_ref.at[b, 0, :, pl.ds(column, GROUP * HEAD)]
+        return pltpu.make_async_copy(source, q_buf.at[w], q_sems.at[w])
+
+    def copy_out(w):
+        if to_pieces:
+            target = out_ref.at[:, pl.ds(out_at + w * HALF, HALF)]
+        else:
+            target = out_ref.at[w, 0, :, pl.ds(out_at, GROUP * HEAD)]
+        return pltpu.make_async_copy(out_buf.at[w], target, out_sems.at[w])
+
+    for w in range(heads * BINS):
+
+        @pl.when((step == 0) & active(w))
+        def _(w=w):
+            copy_q(w).start()
+            for i in range(2 * CHIPS):
+
+                @pl.when(i // 2 <= chip)
+                def _(i=i):
+                    copy(i, w).start()
+
+    working = active(step)
+
+    @pl.when(working)
     def _():
-        for b in range(BINS):
-            for i in range(2 * CHIPS):
-
-                @pl.when(i // 2 <= chip)
-                def _(i=i, b=b):
-                    copy(i, b).start()
+        copy_q(step).wait()
 
     for i in range(2 * CHIPS):
 
-        @pl.when(i // 2 <= chip)
+        @pl.when(working & (i // 2 <= chip))
         def _(i=i):
-            copy(i, item).wait()
+            copy(i, step).wait()
 
     def read_head(head):
         if not from_pieces:
-            return q_ref[0, 0, :, pl.ds(head * HEAD, HEAD)]
-        return jnp.concatenate([q_ref[2 * r + head // HALF, head % HALF] for r in range(PARTS)], axis=0)
+            return q_buf[step, :, pl.ds(head * HEAD, HEAD)]
+        return jnp.concatenate([q_buf[step, 2 * r + head // HALF, head % HALF] for r in range(PARTS)], axis=0)
 
     def write_head(head, rows):
         if to_pieces:
             for r in range(PARTS):
-                out_ref[2 * r + head // HALF, head % HALF] = rows[r * PIECE : (r + 1) * PIECE]
+                out_buf[step, 2 * r + head // HALF, head % HALF] = rows[r * PIECE : (r + 1) * PIECE]
         else:
-            out_ref[0, 0, :, pl.ds(head * HEAD, HEAD)] = rows
+            out_buf[step, :, pl.ds(head * HEAD, HEAD)] = rows
 
     def attend(chips):
-        keys = jnp.concatenate([buffer[i, item, 0] for i in range(2 * chips)], axis=0)
-        values = jnp.concatenate([buffer[i, item, 1] for i in range(2 * chips)], axis=0)
+        keys = jnp.concatenate([buffer[i, step, 0] for i in range(2 * chips)], axis=0)
+        values = jnp.concatenate([buffer[i, step, 1] for i in range(2 * chips)], axis=0)
         t = start + lax.broadcasted_iota(jnp.int32, (WIDTH, WIDTH), 0)
         biases = []
         for i in range(2 * chips):
@@ -158,30 +191,46 @@
             write_head(2 * i, out[:WIDTH])
             write_head(2 * i + 1, out[WIDTH:])
 
-    @pl.when(end <= start)
+    @pl.when(working & (end <= start))
     def _():
-        out_ref[...] = jnp.zeros_like(out_ref)
+        out_buf[step] = jnp.zeros(out_buf.shape[1:], BF16)
 
     for chips in range(1, CHIPS + 1):
 
-        @pl.when((end > start) & (chip == chips - 1))
+        @pl.when(working & (end > start) & (chip == chips - 1))
         def _(chips=chips):
             attend(chips)
 
-
-def attend(lengths, place, q, kv, q_spec, out_spec, out_shape, name, from_pieces=False, to_pieces=True, into=None, head_at=0, weight=1):
-    hbm = pl.BlockSpec(memory_space=pltpu.HBM)
-    pairs = BINS * GROUP * WIDTH * WIDTH * 2 * CHIPS
+    @pl.when(working)
+    def _():
+        copy_out(step).start()
+
+    for w in range(heads * BINS):
+
+        @pl.when((step == heads * BINS - 1) & active(w))
+        def _(w=w):
+            copy_out(w).wait()
+
+
+def attend(lengths, place, q, q_at, kv, out_shape, out_at, name, from_pieces=False, to_pieces=True, into=None, heads=1, weight=1, part=None):
+    hbm, anywhere = pl.BlockSpec(memory_space=pltpu.HBM), pl.BlockSpec(memory_space=pl.ANY)
+    pairs = heads * BINS * GROUP * WIDTH * WIDTH * 2 * CHIPS
+    steps = heads * BINS
+    pieces, columns = (steps, ROWS, HALF, PIECE, HEAD), (steps, WIDTH, GROUP * HEAD)
     return pl.pallas_call(
-        functools.partial(attend_kernel, head_at, from_pieces, to_pieces),
+        functools.partial(attend_kernel, heads, part, q_at, out_at, from_pieces, to_pieces),
         grid_spec=pltpu.PrefetchScalarGridSpec(
             num_scalar_prefetch=2,
-            grid=(BINS,),
-            in_specs=[q_spec] + [hbm] * (2 * CHIPS + (0 if into is None else 1)),
-            out_specs=out_spec,
+            grid=(steps,),
+            in_specs=[anywhere] * (1 + 2 * CHIPS) + [hbm] * (0 if into is None else 1),
+            out_specs=hbm,
             scratch_shapes=[
-                pltpu.VMEM((2 * CHIPS, BINS, 2, WIDTH, HEAD), BF16),
-                pltpu.SemaphoreType.DMA((2 * CHIPS, BINS)),
+                pltpu.VMEM((2 * CHIPS, steps, 2, WIDTH, HEAD), BF16),
+                pltpu.VMEM(pieces if from_pieces else columns, BF16),
+                pltpu.VMEM(pieces if to_pieces else columns, BF16),
+                pltpu.SemaphoreType.DMA((2 * CHIPS, steps)),
+                pltpu.SemaphoreType.DMA((steps,)),
+                pltpu.SemaphoreType.DMA((steps,)),
             ],
         ),
         out_shape=out_shape,
@@ -189,7 +238,13 @@
         cost_estimate=pl.CostEstimate(flops=int(weight * 20 * pairs * HEAD), bytes_accessed=4 << 20, transcendentals=pairs),
         compiler_params=pltpu.CompilerParams(vmem_limit_bytes=VMEM_LIMIT),
         name=name,
-    )(lengths, place, *(pltpu.with_memory_space_constraint(a, pltpu.HBM) for a in (q, *kv)), *(() if into is None else (into,)))
+    )(
+        pltpu.with_memory_space_constraint(lengths, pltpu.HBM),
+        place,
+        pltpu.with_memory_space_constraint(q, pltpu.VMEM if from_pieces else pltpu.HBM),
+        *(pltpu.with_memory_space_constraint(piece, pltpu.VMEM) for piece in kv),
+        *(() if into is None else (into,)),
+    )
 
 
 def forward_kernel(sizes, at, bin_of, r_ref, *refs):
@@ -302,17 +357,13 @@
         columns = [slice(head * HEAD, (head + 1) * HEAD) for head in heads]
         return jnp.stack([a[:, 0, :, c] for c in columns for a in (k, v)])
 
-    def query_spec(head):
-        return pl.BlockSpec((1, 1, WIDTH, GROUP * HEAD), lambda b, *_: (b, 0, 0, head))
-
-    def piece_spec(group):
-        return pl.BlockSpec((ROWS, HALF, PIECE, HEAD), lambda b, *_: (0, group * BINS + b, 0, 0))
+    wide = GROUP * HEAD
 
     near_1 = fetch(key_value([1]))
     got_1 = exchange(pack(lengths, queries, key_rows, bin_value_rows))
     near_23 = fetch(key_value([2, 3], near_1))
 
-    second = attend(lengths, ctx, queries, share(near_1), query_spec(1), piece_spec(0), blocks(36), "attend_1")
+    second = attend(lengths, ctx, queries, wide, share(near_1), blocks(36), 0, "attend_1")
     second = forward(bin_of, got_1, (HALF, 1), second, "forward_0")
     got_2 = exchange(second)
     near_23[1:], _ = lax.optimization_barrier((near_23[1:], second))
@@ -323,20 +374,21 @@
     slot_lengths = jnp.sum(jnp.where(my_bins[:, None, None] == order[None, :, None], all_lengths[None], 0), axis=1).astype(jnp.int32)
 
     pieces_23 = share(near_23)
-    third = attend(lengths, ctx, queries, pieces_23, query_spec(2), piece_spec(0), blocks(48), "attend_2", weight=3)
-    third = attend(lengths, ctx, queries, pieces_23, query_spec(3), piece_spec(1), blocks(48), "attend_3", into=third, head_at=1, weight=3)
+    third = attend(lengths, ctx, queries, 2 * wide, pieces_23, blocks(48), 0, "attend_23_early", heads=2, weight=3, part="early")
+    third, got_2 = lax.optimization_barrier((third, got_2))
+    third = attend(lengths, ctx, queries, 2 * wide, pieces_23, blocks(48), 0, "attend_23_late", heads=2, part="late", into=third)
     third = forward(bin_of, got_2, (HALF,), third, "forward_1")
     third, slot_lengths = lax.optimization_barrier((third, slot_lengths))
     got_3 = exchange(third)
 
     kv_0 = jnp.transpose(got_2[:, 32:].reshape(PARTS, 2, BINS, PIECE, HEAD), (1, 2, 0, 3, 4))
     pieces_0 = share(fetch(kv_0.reshape(2, BINS, WIDTH, HEAD)))
-    full = jax.ShapeDtypeStruct(queries.shape, BF16)
-    out = attend(slot_lengths, ctx, got_2, pieces_0, piece_spec(1), query_spec(0), full, "attend_0", True, False)
+    full = pltpu.HBM(queries.shape, BF16)
 
     fourth = forward(bin_of, got_3, (HALF, HALF), None, "forward_23")
-    fourth, out = lax.optimization_barrier((fourth, out))
+    fourth, pieces_0 = lax.optimization_barrier((fourth, pieces_0))
     got_4 = exchange(fourth)
+    out = attend(slot_lengths, ctx, got_2, 4 * HALF, pieces_0, full, 0, "attend_0", True, False)
     out = place(got_3, (32,), out, GROUP * HEAD, "place_1")
     return place(got_4, (0, 16), out, 2 * GROUP * HEAD, "place_23")
 

time: 163 us -> 159 us (0.975)
  waiting for transfers between devices: 66.6 us -> 59.4 us
  starting transfers between devices: 35.8 us -> 40.8 us
  Pallas kernels: 51.9 us -> 49.1 us
    all_to_all x4, waiting for transfers between devices: 52.7 us -> 46.3 us  [exchange(): return lax.all_to_all(sent, 'dp', split_axis=0, concat_axis=0, tiled=True)]
    all_to_all x4, starting transfers between devices: 21.7 us -> 24.9 us  [exchange(): return lax.all_to_all(sent, 'dp', split_axis=0, concat_axis=0, tiled=True)]
    pallas_call x4, Pallas kernels: 39.2 us -> 36.4 us  [attend(): pl.pallas_call(functools.partial(attend_kernel, heads, part, q_at, out_at...]
    ppermute x9, starting transfers between devices: 12.7 us -> 14.6 us  [fetch(): pieces.append(lax.ppermute(kv, 'ctx', pairs))]
    ppermute x12, waiting for transfers between devices: 3.87 us -> 2.08 us  [share(): lax.ppermute(piece, 'ctx', swap)]
  transfers between devices with their start and end apart: 25 -> 25, of which waited for: 13 -> 10; matrix products, arithmetic and copies ran while one was open for 2% -> 2% of each run, Pallas kernels for 28% -> 22%
where the time goes in v3:
time: 159 us; the launch traced here: 156 us
  waiting for transfers between devices  59.4 us (37%)
  Pallas kernels  49.1 us (31%)
  starting transfers between devices  40.8 us (26%)
  local copies, waits for them, and re-layouts  4.4 us (3%)
    all_to_all x4, waiting for transfers between devices, exchange(): return lax.all_to_all(sent, 'dp', split_axis=0, concat_axis=0, tiled=True)  46.3 us
    pallas_call x4, Pallas kernels, attend(): pl.pallas_call(functools.partial(attend_kernel, heads, part, q_at, out_at...  36.4 us
    all_to_all x4, starting transfers between devices, exchange(): return lax.all_to_all(sent, 'dp', split_axis=0, concat_axis=0, tiled=True)  24.9 us
    ppermute x9, starting transfers between devices, fetch(): pieces.append(lax.ppermute(kv, 'ctx', pairs))  14.6 us
    ppermute x9, waiting for transfers between devices, fetch(): pieces.append(lax.ppermute(kv, 'ctx', pairs))  11 us
    pallas_call x3, Pallas kernels, forward(): pl.pallas_call(functools.partial(forward_kernel, sizes, at), grid_spec=pl...  5.68 us
    pallas_call x2, Pallas kernels, place(): pl.pallas_call(functools.partial(place_kernel, at, column), in_specs=[pl....  4.07 us
  transfers between devices with their start and end apart: 25, of which 10 were waited for; matrix products, arithmetic and copies ran while one was open for 2% of the time, Pallas kernels for 22%

profile of v3, /device:TPU:4, one launch (start us, length us, event | category | flops | bytes accessed | tf_op | source)
XLA Modules:
  0.0 155.6 jit_solution(860387300673804774)
XLA Ops:
  1.6 2.2 %collective-permute-start.6 = (bf16[2,4,128,128]{3,2,1,0:T(8,128)(2,1)S(1)}, bf16[2,4,128,128]{3,2,1,0:T(8,128)(2,1)S(1)}, u32[]{:S(2)}, u32[]{:S(2)}) collective-permute-start(bf16[2,4,128,128]{3,2,1,0:T(8,128)(2,1)S(1)} %pad_maximum_fusion.1.refs_0_), channel_id=1, source_target_pairs={{0,2},{1,3},{2,4},{3,5},{4,6},{5,7},{6,0},{7,1},{8,10},{9,11},{10,... | collective-permute-start | bytes 786440 | tf_op jit(solution)/shard_map/ppermute | solution.py:331
  3.8 3.0 %pack.1 = bf16[16,21,16,128]{3,2,1,0:T(8,128)(2,1)} custom-call(s32[4,3]{1,0:T(4,128)} %lengths.7, bf16[4,1,128,4096]{3,2,1,0:T(8,128)(2,1)} %q_ref.7, bf16[4,1,128,512]{3,2,1,0:T(8,128)(2,1)} %k_ref.1, bf16[4,1,128,512]{3,2,1,0:T(8,128)(2,1)} %v_ref.1), custom_call_target="tpu_custom_call" | custom-call | bytes 4194304 | tf_op jit(solution)/shard_map/pack/pallas_call | solution.py:71
  6.8 8.2 %all-to-all-start = ((bf16[16,21,16,128]{3,2,1,0:T(8,128)(2,1)}), bf16[16,21,16,128]{3,2,1,0:T(8,128)(2,1)S(1)}, u32[]{:S(2)}, u32[]{:S(2)}) async-start(bf16[16,21,16,128]{3,2,1,0:T(8,128)(2,1)} %pack.1), calls=%async_computation | async-start | bytes 2752512 | tf_op jit(solution)/shard_map/all_to_all | solution.py:341
  16.5 2.0 %collective-permute-start.4 = (bf16[4,4,128,128]{3,2,1,0:T(8,128)(2,1)S(1)}, bf16[4,4,128,128]{3,2,1,0:T(8,128)(2,1)S(1)}, u32[]{:S(2)}, u32[]{:S(2)}) collective-permute-start(bf16[4,4,128,128]{3,2,1,0:T(8,128)(2,1)S(1)} %pad_maximum_fusion.refs_0_), channel_id=1, source_target_pairs={{0,6},{1,7},{2,0},{3,1},{4,2},{5,3},{6,4},{7,5},{8,14},{9,15},{10,... | collective-permute-start | bytes 1572872 | tf_op jit(solution)/shard_map/ppermute | solution.py:331
  18.5 2.2 %collective-permute-start.3 = (bf16[4,4,128,128]{3,2,1,0:T(8,128)(2,1)S(1)}, bf16[4,4,128,128]{3,2,1,0:T(8,128)(2,1)}, u32[]{:S(2)}, u32[]{:S(2)}) collective-permute-start(bf16[4,4,128,128]{3,2,1,0:T(8,128)(2,1)S(1)} %pad_maximum_fusion.refs_0_), channel_id=1, source_target_pairs={{0,4},{1,5},{2,6},{3,7},{4,0},{5,1},{6,2},{7,3},{8,12},{9,13},{10,... | collective-permute-start | bytes 1572872 | tf_op jit(solution)/shard_map/ppermute | solution.py:331
  20.7 2.5 %collective-permute-start.2 = (bf16[4,4,128,128]{3,2,1,0:T(8,128)(2,1)S(1)}, bf16[4,4,128,128]{3,2,1,0:T(8,128)(2,1)}, u32[]{:S(2)}, u32[]{:S(2)}) collective-permute-start(bf16[4,4,128,128]{3,2,1,0:T(8,128)(2,1)S(1)} %pad_maximum_fusion.refs_0_), channel_id=1, source_target_pairs={{0,2},{1,3},{2,4},{3,5},{4,6},{5,7},{6,0},{7,1},{8,10},{9,11},{10,... | collective-permute-start | bytes 1572872 | tf_op jit(solution)/shard_map/ppermute | solution.py:331
  23.2 8.8 %attend_1.1.refs_0_ = bf16[16,36,16,128]{3,2,1,0:T(8,128)(2,1)} custom-call(s32[4,3]{1,0:T(4,128)} %lengths.7, s32[1]{0:T(128)} %bitcast.1.place, bf16[4,1,128,4096]{3,2,1,0:T(8,128)(2,1)} %q_ref.7, bf16[2,4,128,128]{3,2,1,0:T(8,128)(2,1)S(1)} %pad_maximum_fusion.1.refs_0_, bf16[2,4,128,128]{3,2,1,0:T(8,128)(2,1)} %collective-permute-done.5.refs_1_, ...), custom_call_target="tpu_custom_call" | custom-call | flops 10737418240 | bytes 4194304 | tf_op jit(solution)/shard_map/attend_1/pallas_call | solution.py:220
  32.0 5.4 %all-to-all-done.r_ref = bf16[16,21,16,128]{3,2,1,0:T(8,128)(2,1)S(1)} async-done(((bf16[16,21,16,128]{3,2,1,0:T(8,128)(2,1)}), bf16[16,21,16,128]{3,2,1,0:T(8,128)(2,1)S(1)}, u32[]{:S(2)}, u32[]{:S(2)}) %all-to-all-start) | async-done | bytes 1376288 | tf_op jit(solution)/shard_map/all_to_all | solution.py:341
  37.5 1.8 %forward_0.1 = bf16[16,36,16,128]{3,2,1,0:T(8,128)(2,1)} custom-call(s32[64]{0:T(128)S(1)} %select_reduce_fusion.bin_of, bf16[16,21,16,128]{3,2,1,0:T(8,128)(2,1)S(1)} %all-to-all-done.r_ref, bf16[16,36,16,128]{3,2,1,0:T(8,128)(2,1)} %attend_1.1.refs_0_), custom_call_target="tpu_custom_call", output_to_operand_aliasing={{}: (2, {})} | custom-call | bytes 4194304 | tf_op jit(solution)/shard_map/forward_0/pallas_call | solution.py:273
  39.3 3.7 %all-to-all-start.1 = ((bf16[16,36,16,128]{3,2,1,0:T(8,128)(2,1)}), bf16[16,36,16,128]{3,2,1,0:T(8,128)(2,1)S(1)}, u32[]{:S(2)}, u32[]{:S(2)}) async-start(bf16[16,36,16,128]{3,2,1,0:T(8,128)(2,1)} %forward_0.1), calls=%async_computation.1 | async-start | bytes 4718592 | tf_op jit(solution)/shard_map/all_to_all | solution.py:341
  43.1 2.2 %collective-permute-done.2.refs_2_ = bf16[4,4,128,128]{3,2,1,0:T(8,128)(2,1)} collective-permute-done((bf16[4,4,128,128]{3,2,1,0:T(8,128)(2,1)S(1)}, bf16[4,4,128,128]{3,2,1,0:T(8,128)(2,1)}, u32[]{:S(2)}, u32[]{:S(2)}) %collective-permute-start.2) | collective-permute-done | bytes 524320 | tf_op jit(solution)/shard_map/ppermute | solution.py:331
  49.1 9.3 %attend_23_early.1.refs_8_ = bf16[16,48,16,128]{3,2,1,0:T(8,128)(2,1)} custom-call(s32[4,3]{1,0:T(4,128)} %lengths.7, s32[1]{0:T(128)} %bitcast.1.place, bf16[4,1,128,4096]{3,2,1,0:T(8,128)(2,1)} %q_ref.7, bf16[4,4,128,128]{3,2,1,0:T(8,128)(2,1)S(1)} %pad_maximum_fusion.refs_0_, bf16[4,4,128,128]{3,2,1,0:T(8,128)(2,1)} %collective-permute-done.1.refs_1_, ...), custom_call_target="tpu_custom_call" | custom-call | flops 64424509440 | bytes 4194304 | tf_op jit(solution)/shard_map/attend_23_early/pallas_call | solution.py:220
  58.4 17.1 %all-to-all-done.1.r_ref.q_ref = bf16[16,36,16,128]{3,2,1,0:T(8,128)(2,1)S(1)} async-done(((bf16[16,36,16,128]{3,2,1,0:T(8,128)(2,1)}), bf16[16,36,16,128]{3,2,1,0:T(8,128)(2,1)S(1)}, u32[]{:S(2)}, u32[]{:S(2)}) %all-to-all-start.1) | async-done | bytes 2359328 | tf_op jit(solution)/shard_map/all_to_all | solution.py:341
  75.6 9.4 %attend_23_late.1.refs_0_ = bf16[16,48,16,128]{3,2,1,0:T(8,128)(2,1)} custom-call(s32[4,3]{1,0:T(4,128)} %lengths.7, s32[1]{0:T(128)} %bitcast.1.place, bf16[4,1,128,4096]{3,2,1,0:T(8,128)(2,1)} %q_ref.7, bf16[4,4,128,128]{3,2,1,0:T(8,128)(2,1)S(1)} %pad_maximum_fusion.refs_0_, ...), custom_call_target="tpu_custom_call", output_to_operand_aliasing={{}: (11, {})} | custom-call | flops 21474836480 | bytes 4194304 | tf_op jit(solution)/shard_map/attend_23_late/pallas_call | solution.py:220
  86.8 4.1 %all-to-all-start.2 = ((bf16[16,48,16,128]{3,2,1,0:T(8,128)(2,1)}), bf16[16,48,16,128]{3,2,1,0:T(8,128)(2,1)S(1)}, u32[]{:S(2)}, u32[]{:S(2)}) async-start(bf16[16,48,16,128]{3,2,1,0:T(8,128)(2,1)} %forward_1.1), calls=%async_computation.2 | async-start | bytes 6291456 | tf_op jit(solution)/shard_map/all_to_all | solution.py:341
  91.6 3.0 %collective-permute-start.19 = (bf16[2,4,128,128]{3,2,1,0:T(8,128)(2,1)}, bf16[2,4,128,128]{3,2,1,0:T(8,128)(2,1)S(1)}, u32[]{:S(2)}, u32[]{:S(2)}) collective-permute-start(bf16[2,4,128,128]{3,2,1,0:T(8,128)(2,1)} %bitcast.15.refs_0_), channel_id=1, source_target_pairs={{0,6},{1,7},{2,0},{3,1},{4,2},{5,3},{6,4},{7,5},{8,14},{9,15},{10,... | collective-permute-start | bytes 786440 | tf_op jit(solution)/shard_map/ppermute | solution.py:331
  96.7 4.9 %collective-permute-done.19.refs_6_ = bf16[2,4,128,128]{3,2,1,0:T(8,128)(2,1)S(1)} collective-permute-done((bf16[2,4,128,128]{3,2,1,0:T(8,128)(2,1)}, bf16[2,4,128,128]{3,2,1,0:T(8,128)(2,1)S(1)}, u32[]{:S(2)}, u32[]{:S(2)}) %collective-permute-start.19) | collective-permute-done | bytes 262176 | tf_op jit(solution)/shard_map/ppermute | solution.py:331
  102.9 2.5 %collective-permute-done.15.refs_2_ = bf16[2,4,128,128]{3,2,1,0:T(8,128)(2,1)} collective-permute-done((bf16[2,4,128,128]{3,2,1,0:T(8,128)(2,1)}, bf16[2,4,128,128]{3,2,1,0:T(8,128)(2,1)}, u32[]{:S(2)}, u32[]{:S(2)}) %collective-permute-start.15) | collective-permute-done | bytes 262176 | tf_op jit(solution)/shard_map/ppermute | solution.py:331
  105.5 15.0 %all-to-all-done.2.r_ref = bf16[16,48,16,128]{3,2,1,0:T(8,128)(2,1)S(1)} async-done(((bf16[16,48,16,128]{3,2,1,0:T(8,128)(2,1)}), bf16[16,48,16,128]{3,2,1,0:T(8,128)(2,1)S(1)}, u32[]{:S(2)}, u32[]{:S(2)}) %all-to-all-start.2) | async-done | bytes 3145760 | tf_op jit(solution)/shard_map/all_to_all | solution.py:341
  120.5 2.1 %forward_23.1 = bf16[16,32,16,128]{3,2,1,0:T(8,128)(2,1)} custom-call(s32[64]{0:T(128)S(1)} %select_reduce_fusion.bin_of, bf16[16,48,16,128]{3,2,1,0:T(8,128)(2,1)S(1)} %all-to-all-done.2.r_ref), custom_call_target="tpu_custom_call" | custom-call | bytes 4194304 | tf_op jit(solution)/shard_map/forward_23/pallas_call | solution.py:273
  122.6 8.9 %all-to-all-start.3 = ((bf16[16,32,16,128]{3,2,1,0:T(8,128)(2,1)}), bf16[16,32,16,128]{3,2,1,0:T(8,128)(2,1)}, u32[]{:S(2)}, u32[]{:S(2)}) async-start(bf16[16,32,16,128]{3,2,1,0:T(8,128)(2,1)} %forward_23.1), calls=%async_computation.3 | async-start | bytes 4194304 | tf_op jit(solution)/shard_map/all_to_all | solution.py:341
  133.9 8.8 %attend_0.1._ = bf16[4,1,128,4096]{3,2,1,0:T(8,128)(2,1)} custom-call(s32[4,3]{1,0:T(4,128)} %copy.33.lengths, s32[1]{0:T(128)} %bitcast.1.place, bf16[16,36,16,128]{3,2,1,0:T(8,128)(2,1)S(1)} %copy-done.1, bf16[2,4,128,128]{3,2,1,0:T(8,128)(2,1)} %bitcast.15.refs_0_, bf16[2,4,128,128]{3,2,1,0:T(8,128)(2,1)} %collective-permute-done.14.refs_1_, ...), custom_call_target="tpu_custom_call" | custom-call | flops 10737418240 | bytes 4194304 | tf_op jit(solution)/shard_map/attend_0/pallas_call | solution.py:220
  143.8 8.7 %all-to-all-done.3.r_ref = bf16[16,32,16,128]{3,2,1,0:T(8,128)(2,1)} async-done(((bf16[16,32,16,128]{3,2,1,0:T(8,128)(2,1)}), bf16[16,32,16,128]{3,2,1,0:T(8,128)(2,1)}, u32[]{:S(2)}, u32[]{:S(2)}) %all-to-all-start.3) | async-done | bytes 2097184 | tf_op jit(solution)/shard_map/all_to_all | solution.py:341
  152.4 3.0 %place_23.1 = bf16[4,1,128,4096]{3,2,1,0:T(8,128)(2,1)} custom-call(bf16[16,32,16,128]{3,2,1,0:T(8,128)(2,1)} %all-to-all-done.3.r_ref, bf16[4,1,128,4096]{3,2,1,0:T(8,128)(2,1)} %place_1.1._), custom_call_target="tpu_custom_call", output_to_operand_aliasing={{}: (1, {})} | custom-call | bytes 4194304 | tf_op jit(solution)/shard_map/place_23/pallas_call | solution.py:311
  (67 shorter events, 16.0 us)
Async XLA Ops:
  1.1 14.6 %collective-permute-start.8 = (bf16[2,4,128,128]{3,2,1,0:T(8,128)(2,1)S(1)}, bf16[2,4,128,128]{3,2,1,0:T(8,128)(2,1)S(1)}, u32[]{:S(2)}, u32[]{:S(2)}) collective-permute-start(bf16[2,4,128,128]{3,2,1,0:T(8,128)(2,1)S(1)} %pad_maximum_fusion.1.refs_0_), channel_id=1, source_target_pairs={{0,4},{1,5},{2,6},{3,7},{4,0},{5,1},{6,2},{7,3},{8,12},{9,13},{10,... | collective-permute-start | bytes 786440 | tf_op jit(solution)/shard_map/ppermute | solution.py:331
  1.6 14.5 %collective-permute-start.6 = (bf16[2,4,128,128]{3,2,1,0:T(8,128)(2,1)S(1)}, bf16[2,4,128,128]{3,2,1,0:T(8,128)(2,1)S(1)}, u32[]{:S(2)}, u32[]{:S(2)}) collective-permute-start(bf16[2,4,128,128]{3,2,1,0:T(8,128)(2,1)S(1)} %pad_maximum_fusion.1.refs_0_), channel_id=1, source_target_pairs={{0,2},{1,3},{2,4},{3,5},{4,6},{5,7},{6,0},{7,1},{8,10},{9,11},{10,... | collective-permute-start | bytes 786440 | tf_op jit(solution)/shard_map/ppermute | solution.py:331
  3.7 14.7 %collective-permute-start.5 = (bf16[2,4,128,128]{3,2,1,0:T(8,128)(2,1)S(1)}, bf16[2,4,128,128]{3,2,1,0:T(8,128)(2,1)}, u32[]{:S(2)}, u32[]{:S(2)}) collective-permute-start(bf16[2,4,128,128]{3,2,1,0:T(8,128)(2,1)S(1)} %pad_maximum_fusion.1.refs_0_), channel_id=1, source_target_pairs={{0,1},{1,0},{2,3},{3,2},{4,5},{5,4},{6,7},{7,6},{8,9},{9,8},{10,11... | collective-permute-start | bytes 786440 | tf_op jit(solution)/shard_map/ppermute | solution.py:337
  3.7 11.8 %collective-permute-start = (bf16[2,4,128,128]{3,2,1,0:T(8,128)(2,1)S(1)}, bf16[2,4,128,128]{3,2,1,0:T(8,128)(2,1)}, u32[]{:S(2)}, u32[]{:S(2)}) collective-permute-start(bf16[2,4,128,128]{3,2,1,0:T(8,128)(2,1)S(1)} %pad_maximum_fusion.1.refs_0_), channel_id=1, source_target_pairs={{0,6},{1,7},{2,0},{3,1},{4,2},{5,3},{6,4},{7,5},{8,14},{9,15},{10,... | collective-permute-start | bytes 786440 | tf_op jit(solution)/shard_map/ppermute | solution.py:331
  6.8 30.7 %all-to-all-start = ((bf16[16,21,16,128]{3,2,1,0:T(8,128)(2,1)}), bf16[16,21,16,128]{3,2,1,0:T(8,128)(2,1)S(1)}, u32[]{:S(2)}, u32[]{:S(2)}) async-start(bf16[16,21,16,128]{3,2,1,0:T(8,128)(2,1)} %pack.1), calls=%async_computation | async-start | bytes 2752512 | tf_op jit(solution)/shard_map/all_to_all | solution.py:341
  15.5 7.7 %collective-permute-start.10 = (bf16[2,4,128,128]{3,2,1,0:T(8,128)(2,1)}, bf16[2,4,128,128]{3,2,1,0:T(8,128)(2,1)S(1)}, u32[]{:S(2)}, u32[]{:S(2)}) collective-permute-start(bf16[2,4,128,128]{3,2,1,0:T(8,128)(2,1)} %collective-permute-done.refs_6_), channel_id=1, source_target_pairs={{0,1},{1,0},{2,3},{3,2},{4,5},{5,4},{6,7},{7,6},{8,9},{9,8},{10,11... | collective-permute-start | bytes 786440 | tf_op jit(solution)/shard_map/ppermute | solution.py:337
  15.7 5.0 %collective-permute-start.9 = (bf16[2,4,128,128]{3,2,1,0:T(8,128)(2,1)S(1)}, bf16[2,4,128,128]{3,2,1,0:T(8,128)(2,1)S(1)}, u32[]{:S(2)}, u32[]{:S(2)}) collective-permute-start(bf16[2,4,128,128]{3,2,1,0:T(8,128)(2,1)S(1)} %collective-permute-done.8.refs_4_), channel_id=1, source_target_pairs={{0,1},{1,0},{2,3},{3,2},{4,5},{5,4},{6,7},{7,6},{8,9},{9,8},{10,11... | collective-permute-start | bytes 786440 | tf_op jit(solution)/shard_map/ppermute | solution.py:337
  16.1 7.1 %collective-permute-start.7 = (bf16[2,4,128,128]{3,2,1,0:T(8,128)(2,1)S(1)}, bf16[2,4,128,128]{3,2,1,0:T(8,128)(2,1)S(1)}, u32[]{:S(2)}, u32[]{:S(2)}) collective-permute-start(bf16[2,4,128,128]{3,2,1,0:T(8,128)(2,1)S(1)} %collective-permute-done.6.refs_2_), channel_id=1, source_target_pairs={{0,1},{1,0},{2,3},{3,2},{4,5},{5,4},{6,7},{7,6},{8,9},{9,8},{10,11... | collective-permute-start | bytes 786440 | tf_op jit(solution)/shard_map/ppermute | solution.py:337
  16.5 26.6 %collective-permute-start.4 = (bf16[4,4,128,128]{3,2,1,0:T(8,128)(2,1)S(1)}, bf16[4,4,128,128]{3,2,1,0:T(8,128)(2,1)S(1)}, u32[]{:S(2)}, u32[]{:S(2)}) collective-permute-start(bf16[4,4,128,128]{3,2,1,0:T(8,128)(2,1)S(1)} %pad_maximum_fusion.refs_0_), channel_id=1, source_target_pairs={{0,6},{1,7},{2,0},{3,1},{4,2},{5,3},{6,4},{7,5},{8,14},{9,15},{10,... | collective-permute-start | bytes 1572872 | tf_op jit(solution)/shard_map/ppermute | solution.py:331
  18.5 24.6 %collective-permute-start.3 = (bf16[4,4,128,128]{3,2,1,0:T(8,128)(2,1)S(1)}, bf16[4,4,128,128]{3,2,1,0:T(8,128)(2,1)}, u32[]{:S(2)}, u32[]{:S(2)}) collective-permute-start(bf16[4,4,128,128]{3,2,1,0:T(8,128)(2,1)S(1)} %pad_maximum_fusion.refs_0_), channel_id=1, source_target_pairs={{0,4},{1,5},{2,6},{3,7},{4,0},{5,1},{6,2},{7,3},{8,12},{9,13},{10,... | collective-permute-start | bytes 1572872 | tf_op jit(solution)/shard_map/ppermute | solution.py:331
  20.7 24.6 %collective-permute-start.2 = (bf16[4,4,128,128]{3,2,1,0:T(8,128)(2,1)S(1)}, bf16[4,4,128,128]{3,2,1,0:T(8,128)(2,1)}, u32[]{:S(2)}, u32[]{:S(2)}) collective-permute-start(bf16[4,4,128,128]{3,2,1,0:T(8,128)(2,1)S(1)} %pad_maximum_fusion.refs_0_), channel_id=1, source_target_pairs={{0,2},{1,3},{2,4},{3,5},{4,6},{5,7},{6,0},{7,1},{8,10},{9,11},{10,... | collective-permute-start | bytes 1572872 | tf_op jit(solution)/shard_map/ppermute | solution.py:331
  23.2 23.8 %collective-permute-start.1 = (bf16[4,4,128,128]{3,2,1,0:T(8,128)(2,1)S(1)}, bf16[4,4,128,128]{3,2,1,0:T(8,128)(2,1)}, u32[]{:S(2)}, u32[]{:S(2)}) collective-permute-start(bf16[4,4,128,128]{3,2,1,0:T(8,128)(2,1)S(1)} %pad_maximum_fusion.refs_0_), channel_id=1, source_target_pairs={{0,1},{1,0},{2,3},{3,2},{4,5},{5,4},{6,7},{7,6},{8,9},{9,8},{10,11... | collective-permute-start | bytes 1572872 | tf_op jit(solution)/shard_map/ppermute | solution.py:337
  39.3 36.2 %all-to-all-start.1 = ((bf16[16,36,16,128]{3,2,1,0:T(8,128)(2,1)}), bf16[16,36,16,128]{3,2,1,0:T(8,128)(2,1)S(1)}, u32[]{:S(2)}, u32[]{:S(2)}) async-start(bf16[16,36,16,128]{3,2,1,0:T(8,128)(2,1)} %forward_0.1), calls=%async_computation.1 | async-start | bytes 4718592 | tf_op jit(solution)/shard_map/all_to_all | solution.py:341
  45.3 3.7 %collective-permute-start.12 = (bf16[4,4,128,128]{3,2,1,0:T(8,128)(2,1)}, bf16[4,4,128,128]{3,2,1,0:T(8,128)(2,1)}, u32[]{:S(2)}, u32[]{:S(2)}) collective-permute-start(bf16[4,4,128,128]{3,2,1,0:T(8,128)(2,1)} %collective-permute-done.3.refs_4_), channel_id=1, source_target_pairs={{0,1},{1,0},{2,3},{3,2},{4,5},{5,4},{6,7},{7,6},{8,9},{9,8},{10,11... | collective-permute-start | bytes 1572872 | tf_op jit(solution)/shard_map/ppermute | solution.py:337
  45.8 3.2 %collective-permute-start.13 = (bf16[4,4,128,128]{3,2,1,0:T(8,128)(2,1)S(1)}, bf16[4,4,128,128]{3,2,1,0:T(8,128)(2,1)}, u32[]{:S(2)}, u32[]{:S(2)}) collective-permute-start(bf16[4,4,128,128]{3,2,1,0:T(8,128)(2,1)S(1)} %collective-permute-done.4.refs_6_), channel_id=1, source_target_pairs={{0,1},{1,0},{2,3},{3,2},{4,5},{5,4},{6,7},{7,6},{8,9},{9,8},{10,11... | collective-permute-start | bytes 1572872 | tf_op jit(solution)/shard_map/ppermute | solution.py:337
  86.8 33.7 %all-to-all-start.2 = ((bf16[16,48,16,128]{3,2,1,0:T(8,128)(2,1)}), bf16[16,48,16,128]{3,2,1,0:T(8,128)(2,1)S(1)}, u32[]{:S(2)}, u32[]{:S(2)}) async-start(bf16[16,48,16,128]{3,2,1,0:T(8,128)(2,1)} %forward_1.1), calls=%async_computation.2 | async-start | bytes 6291456 | tf_op jit(solution)/shard_map/all_to_all | solution.py:341
  91.6 10.0 %collective-permute-start.19 = (bf16[2,4,128,128]{3,2,1,0:T(8,128)(2,1)}, bf16[2,4,128,128]{3,2,1,0:T(8,128)(2,1)S(1)}, u32[]{:S(2)}, u32[]{:S(2)}) collective-permute-start(bf16[2,4,128,128]{3,2,1,0:T(8,128)(2,1)} %bitcast.15.refs_0_), channel_id=1, source_target_pairs={{0,6},{1,7},{2,0},{3,1},{4,2},{5,3},{6,4},{7,5},{8,14},{9,15},{10,... | collective-permute-start | bytes 786440 | tf_op jit(solution)/shard_map/ppermute | solution.py:331
  94.6 8.3 %collective-permute-start.17 = (bf16[2,4,128,128]{3,2,1,0:T(8,128)(2,1)}, bf16[2,4,128,128]{3,2,1,0:T(8,128)(2,1)}, u32[]{:S(2)}, u32[]{:S(2)}) collective-permute-start(bf16[2,4,128,128]{3,2,1,0:T(8,128)(2,1)} %bitcast.15.refs_0_), channel_id=1, source_target_pairs={{0,4},{1,5},{2,6},{3,7},{4,0},{5,1},{6,2},{7,3},{8,12},{9,13},{10,... | collective-permute-start | bytes 786440 | tf_op jit(solution)/shard_map/ppermute | solution.py:331
  96.0 9.5 %collective-permute-start.15 = (bf16[2,4,128,128]{3,2,1,0:T(8,128)(2,1)}, bf16[2,4,128,128]{3,2,1,0:T(8,128)(2,1)}, u32[]{:S(2)}, u32[]{:S(2)}) collective-permute-start(bf16[2,4,128,128]{3,2,1,0:T(8,128)(2,1)} %bitcast.15.refs_0_), channel_id=1, source_target_pairs={{0,2},{1,3},{2,4},{3,5},{4,6},{5,7},{6,0},{7,1},{8,10},{9,11},{10,... | collective-permute-start | bytes 786440 | tf_op jit(solution)/shard_map/ppermute | solution.py:331
  96.7 25.9 %collective-permute-start.14 = (bf16[2,4,128,128]{3,2,1,0:T(8,128)(2,1)}, bf16[2,4,128,128]{3,2,1,0:T(8,128)(2,1)}, u32[]{:S(2)}, u32[]{:S(2)}) collective-permute-start(bf16[2,4,128,128]{3,2,1,0:T(8,128)(2,1)} %bitcast.15.refs_0_), channel_id=1, source_target_pairs={{0,1},{1,0},{2,3},{3,2},{4,5},{5,4},{6,7},{7,6},{8,9},{9,8},{10,11... | collective-permute-start | bytes 786440 | tf_op jit(solution)/shard_map/ppermute | solution.py:337
  101.7 21.0 %collective-permute-start.20 = (bf16[2,4,128,128]{3,2,1,0:T(8,128)(2,1)S(1)}, bf16[2,4,128,128]{3,2,1,0:T(8,128)(2,1)}, u32[]{:S(2)}, u32[]{:S(2)}) collective-permute-start(bf16[2,4,128,128]{3,2,1,0:T(8,128)(2,1)S(1)} %collective-permute-done.19.refs_6_), channel_id=1, source_target_pairs={{0,1},{1,0},{2,3},{3,2},{4,5},{5,4},{6,7},{7,6},{8,9},{9,8},{10,11... | collective-permute-start | bytes 786440 | tf_op jit(solution)/shard_map/ppermute | solution.py:337
  102.9 19.7 %collective-permute-start.18 = (bf16[2,4,128,128]{3,2,1,0:T(8,128)(2,1)}, bf16[2,4,128,128]{3,2,1,0:T(8,128)(2,1)}, u32[]{:S(2)}, u32[]{:S(2)}) collective-permute-start(bf16[2,4,128,128]{3,2,1,0:T(8,128)(2,1)} %collective-permute-done.17.refs_4_), channel_id=1, source_target_pairs={{0,1},{1,0},{2,3},{3,2},{4,5},{5,4},{6,7},{7,6},{8,9},{9,8},{10,11... | collective-permute-start | bytes 786440 | tf_op jit(solution)/shard_map/ppermute | solution.py:337
  105.5 17.2 %collective-permute-start.16 = (bf16[2,4,128,128]{3,2,1,0:T(8,128)(2,1)}, bf16[2,4,128,128]{3,2,1,0:T(8,128)(2,1)}, u32[]{:S(2)}, u32[]{:S(2)}) collective-permute-start(bf16[2,4,128,128]{3,2,1,0:T(8,128)(2,1)} %collective-permute-done.15.refs_2_), channel_id=1, source_target_pairs={{0,1},{1,0},{2,3},{3,2},{4,5},{5,4},{6,7},{7,6},{8,9},{9,8},{10,11... | collective-permute-start | bytes 786440 | tf_op jit(solution)/shard_map/ppermute | solution.py:337
  122.6 29.8 %all-to-all-start.3 = ((bf16[16,32,16,128]{3,2,1,0:T(8,128)(2,1)}), bf16[16,32,16,128]{3,2,1,0:T(8,128)(2,1)}, u32[]{:S(2)}, u32[]{:S(2)}) async-start(bf16[16,32,16,128]{3,2,1,0:T(8,128)(2,1)} %forward_23.1), calls=%async_computation.3 | async-start | bytes 4194304 | tf_op jit(solution)/shard_map/all_to_all | solution.py:341
  (8 other events, 57.8 us)
